TPU v7x, 256 devices: a whole 4x4x8 slice. The times are simulated.
256 devices in a mesh: dp: 64 (over x, y, z_lo), grp: 4 (over z_hi, core).
Axes of the slice: x: 4, y: 4, z: 8 (z_hi: 2, z_lo: 4; z = z_hi * 4 + z_lo), core: 2. Of those that a mesh axis runs over, the one named last changes fastest.
Arguments:
- acts: bfloat16 [32768, 5120], P(('dp', 'grp')), may hold values from -6 to 6
- grads: bfloat16 [32768, 5120], P(('dp', 'grp')), may hold values from -6 to 6
- basis_a: bfloat16 [8, 640, 640], P(None, 'grp'), may hold values from -0.25 to 0.25
- basis_g: bfloat16 [8, 640, 640], P(None, 'grp'), may hold values from -0.25 to 0.25
- eig_a: float32 [8, 640], replicated, may hold values from 0.3 to 3
- eig_g: float32 [8, 640], replicated, may hold values from 0.3 to 3
Outputs:
- factor_a: float32 [5120, 640], P(('dp', 'grp'))
- factor_g: float32 [5120, 640], P(('dp', 'grp'))
- precond: bfloat16 [64, 640, 640], P('dp', None, 'grp')
All inputs are finite; a program needn't handle non-finite values.
Results may differ from a plain program's by a relative error of at most 0.022.
Values may be sent and summed in bfloat16 or wider, within the bound.
No kernel may reach another device: no remote copies, remote signals or barrier semaphores. Data moves between devices by JAX's collectives and lax.ppermute only.
A program may use at most 128 MiB of HBM per device.

v0:
```python
import jax
import jax.numpy as jnp
from jax import lax
from jax.experimental import pallas as pl
from jax.experimental.pallas import tpu as pltpu
from jax.sharding import Mesh, PartitionSpec as P

DAMPING = 0.03
ROWS = (((0,), (0,)), ((), ()))
COLS = (((1,), (1,)), ((), ()))
MIB = 1 << 20
F32 = jnp.float32
BF16 = jnp.bfloat16
VMEM = pl.BlockSpec(memory_space=pltpu.VMEM)
SMEM = pl.BlockSpec(memory_space=pltpu.SMEM)
PLACE = (0, 4, 1, 5, 3, 7, 2, 6)
CHIP = (0, 7, 1, 2, 3, 4, 6, 5)
DISTANCE = (0, 2, 6, 4, 1, 3, 7, 5)
TAKES = tuple(CHIP.index(i) for i in range(8))


def shift(count, by):
    return [(i, (i + by) % count) for i in range(count)]


def z_shift(by):
    at = [(z % 4) * 2 + z // 4 for z in range(8)]
    return [(at[z], at[(z + by) % 8]) for z in range(8)]


def to_z(array, by):
    return lax.ppermute(array, ("zl", "zh"), z_shift(by))


def swap(array, axis="core"):
    return lax.ppermute(array, axis, shift(2, 1))


def params(mib=24):
    return pltpu.CompilerParams(vmem_limit_bytes=mib * MIB)


def exchange(plans, count, width):
    pieces = [[None] * count for _ in plans]
    for d in (2, 1, 3, 0):
        for (array, axis), got in zip(plans, pieces):
            first = lax.rem(lax.axis_index(axis) + d, count) * width
            cols = lax.dynamic_slice_in_dim(array, first, width, 1)
            got[d] = cols if d == 0 else lax.ppermute(cols, axis, shift(count, d))
    return [jnp.concatenate(got, axis=0) for got in pieces]


def gather_near(own, axis):
    return own, lax.ppermute(own, axis, shift(4, 1)), lax.ppermute(own, axis, shift(4, 3))


def gather_far(near, axis):
    _, back, ahead = near
    half = back.shape[0] // 2
    return (
        lax.ppermute(back[:half], axis, shift(4, 1)),
        lax.ppermute(ahead[half:], axis, shift(4, 3)),
    )


def rows_of(near, outer, inner, cols):
    return near[(0, 1, None, 2)[outer]][inner * 128 : inner * 128 + 128, cols]


def block(i):
    return slice(i * 640, i * 640 + 640)


def product(left, right):
    return lax.dot_general(left, right, ROWS, preferred_element_type=F32)


def factor_rows(where_ref, acts_slab, grads_slab):
    y, x = where_ref[3], where_ref[4]
    base = pl.multiple_of((y // 2) * 640, 128)
    window = pl.multiple_of((y // 2) * 640 + (y % 2) * 256, 128)
    parts = [product(acts_slab(pl.ds(window, 384)), acts_slab(pl.ds(base, 640)))]
    for c in range(2):
        window = pl.multiple_of(c * 640 + x * 128, 128)
        parts.append(product(grads_slab(pl.ds(window, 256)), grads_slab(block(c))))
    return jnp.concatenate(parts, axis=0)


def near_kernel(where_ref, *refs):
    acts, grads = refs[:3], refs[3:6]
    total_ref, factor_ref, acts_mid_ref, grads_mid_ref = refs[6:]
    pairs = [(e, d) for e in (0, 1, 3) for d in (0, 1, 3)]

    def acts_slab(cols):
        return jnp.concatenate([rows_of(acts, e, d, cols) for e, d in pairs], axis=0)

    def grads_slab(cols):
        return jnp.concatenate([rows_of(grads, d, e, cols) for e, d in pairs], axis=0)

    for i, outer in enumerate((0, 1, 3)):
        acts_mid_ref[i * 128 : i * 128 + 128] = rows_of(acts, outer, 2, slice(None))
        grads_mid_ref[i * 128 : i * 128 + 128] = rows_of(grads, outer, 2, slice(None))
    for c in range(2):
        total_ref[c] = product(grads_slab(block(c)), acts_slab(slice(None)))
    factor_ref[...] = factor_rows(where_ref, acts_slab, grads_slab)


def far_kernel(
    where_ref, acts_mid, grads_mid, al, ah, gl, gh, total_ref, factor_ref, order_ref, keep_ref, send_ref
):
    z, core, start = where_ref[0], where_ref[1], where_ref[2]

    def acts_slab(cols):
        return jnp.concatenate(
            [acts_mid[:, cols], al[:, cols], ah[128:256, cols], ah[0:128, cols]], axis=0
        )

    def grads_slab(cols):
        return jnp.concatenate(
            [gl[:, cols], gh[128:256, cols], grads_mid[:, cols], gh[0:128, cols]], axis=0
        )

    for c in range(2):
        total = total_ref[c] + product(grads_slab(block(c)), acts_slab(slice(None)))
        for b in range(2):
            for q in range(4):
                away = lax.rem(CHIP[4 * b + 2 * c + q // 2] + start - z + 8, 8)
                place = 0
                for d in range(8):
                    place = jnp.where(away == d, PLACE[d], place)
                piece = total[q * 160 : q * 160 + 160, block(b)].astype(BF16)

                @pl.when(core == q % 2)
                def _():
                    keep_ref[place, 0:160] = piece

                @pl.when(core != q % 2)
                def _():
                    send_ref[place, 0:160] = piece

    factors = (factor_ref[...] + factor_rows(where_ref, acts_slab, grads_slab)).astype(BF16)
    ordered = jnp.dot(order_ref[...], factors, preferred_element_type=F32).astype(BF16)
    for i in range(8):
        keep_ref[i, 160:208] = ordered[i * 48 : i * 48 + 48]
        send_ref[i, 160:208] = ordered[384 + i * 48 : 384 + i * 48 + 48]


def ordered_rows(x, y, z, core, takes):
    row = jnp.arange(48)
    wanted = []
    for k in (core, 1 - core):
        for d in DISTANCE:
            chip = lax.rem(z + d, 8)
            number = takes(chip)
            of_a = (y % 2) * 64 + 20 * (chip % 4 * 4 + chip // 4 * 2 + k) + row
            of_g = 384 + number // 2 % 2 * 256 + x * 32 + number // 4 * 80
            of_g = of_g + (number % 2 * 2 + k) * 20 + row - 24
            wanted.append(
                jnp.where(row < 20, of_a, jnp.where((row >= 24) & (row < 44), of_g, -1))
            )
    return (jnp.concatenate(wanted)[:, None] == jnp.arange(896)[None, :]).astype(BF16)


def core_sum_kernel(keep, came, here, two, six, to_next, to_prev, up, down):
    def piece(i):
        return (keep[i].astype(F32) + came[i].astype(F32)).astype(BF16)

    here[...] = piece(0)
    two[...] = piece(1)
    six[...] = piece(2)
    opposite = piece(3)
    up[...] = opposite[:96]
    down[...] = opposite[96:]
    for i in range(2):
        to_next[i] = piece(4 + i)
        to_prev[i] = piece(6 + i)


def parity_sum_kernel(two, six, prev, after, up, down, ahead, behind):
    total = two[...].astype(F32) + prev[1].astype(F32)
    ahead[0:96] = (total[:96] + up[...].astype(F32)).astype(BF16)
    ahead[96:208] = total[96:].astype(BF16)
    total = six[...].astype(F32) + after[1].astype(F32)
    behind[0:96] = total[:96].astype(BF16)
    behind[96:208] = (total[96:] + down[...].astype(F32)).astype(BF16)


def left_kernel(here, prev, after, ahead, behind, qa_ref, left_ref, fa_ref, fg_ref):
    total = here[...].astype(F32) + prev[0].astype(F32) + after[0].astype(F32)
    total += ahead[...].astype(F32) + behind[...].astype(F32)
    wgrad = (total[:160] / 128).astype(BF16)
    qa = qa_ref[...].reshape(640, 640)
    left_ref[...] = jnp.dot(wgrad, qa, preferred_element_type=F32).astype(BF16)
    fa_ref[...] = total[160:180] / 32768
    fg_ref[...] = total[184:204] / 32768


def finish_kernel(l0, l1, l2, l3, qg_ref, qa_ref, eig_a_ref, eig_g_ref, out_ref):
    rotated = None
    for r, left in enumerate((l0, l1, l2, l3)):
        part = product(qg_ref[r], left[...])
        rotated = part if rotated is None else rotated + part
    scaled = (rotated / (eig_g_ref[...] * eig_a_ref[...] + DAMPING)).astype(BF16)
    right = jnp.dot(qg_ref[0], scaled, preferred_element_type=F32).astype(BF16)
    qa = qa_ref[...].reshape(640, 640)
    out_ref[...] = lax.dot_general(right, qa, COLS, preferred_element_type=F32).astype(BF16)


def call(kernel, out_shapes, operands, flops, moved, scalars=None):
    shapes = [jax.ShapeDtypeStruct(*o) for o in out_shapes]
    out = pl.pallas_call(
        kernel,
        out_shape=shapes,
        in_specs=([] if scalars is None else [SMEM]) + [VMEM] * len(operands),
        out_specs=[VMEM] * len(shapes),
        compiler_params=params(),
        cost_estimate=pl.CostEstimate(flops=flops, bytes_accessed=moved, transcendentals=0),
    )(*([] if scalars is None else [jnp.stack(scalars).astype(jnp.int32)]), *operands)
    return out if len(out) > 1 else out[0]


def body(acts, grads, basis_a, basis_g, eig_a, eig_g):
    x, y, zl, zh, core = (lax.axis_index(n) for n in ("x", "y", "zl", "zh", "core"))
    z = 4 * zh + zl
    start = 2 * (y % 2)

    def takes(chip):
        number = lax.rem(chip - start + 8, 8)
        found = 0
        for i in range(8):
            found = jnp.where(number == i, TAKES[i], found)
        return found

    mine, theirs = takes(z), takes(lax.rem(z + 4, 8))
    block_a, block_g = 2 * x + mine // 4, 2 * y + mine // 2 % 2
    quarter = 2 * (mine % 2) + core

    def basis_pair(piece):
        return jnp.stack(
            [
                lax.dynamic_index_in_dim(basis_a, 2 * x + piece // 4, 0, keepdims=False),
                lax.dynamic_index_in_dim(basis_g, 2 * y + piece // 2 % 2, 0, keepdims=False),
            ]
        )

    acts_own, grads_own = exchange([(acts, "x"), (grads, "y")], 4, 1280)
    basis_out, acts_own = lax.optimization_barrier((basis_pair(theirs), acts_own))
    basis_far = swap(basis_out, "zh")
    near = (*gather_near(acts_own, "y"), *gather_near(grads_own, "x"))
    acts_far, grads_far = gather_far(near[:3], "y"), gather_far(near[3:], "x")
    order = ordered_rows(x, y, z, core, takes)

    *near, basis_far, order = lax.optimization_barrier((*near, basis_far, order))

    where = (z, core, start, y, x)
    mid = ((384, 1280), BF16)
    total, factor_part, acts_mid, grads_mid = call(
        near_kernel,
        [((2, 640, 1280), F32), ((896, 640), F32), mid, mid],
        near,
        5 * 10**9,
        10**7,
        where,
    )
    w_keep, w_send = call(
        far_kernel,
        [((8, 208, 640), BF16)] * 2,
        (acts_mid, grads_mid, *acts_far, *grads_far, total, factor_part, order),
        4 * 10**9,
        10**7,
        where,
    )
    one, both = ((208, 640), BF16), ((2, 208, 640), BF16)
    own, two, six, to_next, to_prev, up, down = call(
        core_sum_kernel,
        [one, one, one, both, both, ((96, 640), BF16), ((112, 640), BF16)],
        (w_keep, swap(w_send)),
        10**6,
        4 * 10**6,
    )
    basis_far, to_next = lax.optimization_barrier((basis_far, to_next))

    here = jnp.stack([basis_pair(mine), basis_far])
    sibling = swap(here)
    by_core = jnp.where(core == 0, jnp.stack([here, sibling], 1), jnp.stack([sibling, here], 1))
    whole = jnp.where(zh == 0, by_core, by_core[::-1])
    qa = whole[:, :, 0].reshape(4, 160, 640)
    qg = whole[:, :, 1].reshape(4, 160, 640)
    qg = jnp.stack(
        [lax.dynamic_index_in_dim(qg, quarter ^ r, 0, keepdims=False) for r in range(4)]
    )

    prev, after = to_z(to_next, 1), to_z(to_prev, 7)
    up, down = to_z(up, 2), to_z(down, 6)
    ahead, behind = call(
        parity_sum_kernel, [one, one], (two, six, prev, after, up, down), 10**6, 10**6
    )
    ahead, behind = to_z(ahead, 2), to_z(behind, 6)
    left, factor_a, factor_g = call(
        left_kernel,
        [((160, 640), BF16), ((20, 640), F32), ((20, 640), F32)],
        (own, prev, after, ahead, behind, qa),
        10**8,
        3 * 10**6,
    )

    pairs, moves = [], []
    for y0 in range(4):
        for number in range(8):
            b, c, h = number // 4, number // 2 % 2, number % 2
            z0, z1 = ((CHIP[n] + 2 * (y0 % 2)) % 8 for n in (number, number ^ 1))
            at = (y0 * 4 + z0 % 4) * 2 + z0 // 4
            pairs.append((at, (y0 * 4 + z1 % 4) * 2 + z1 // 4))
            moves.append((at, ((2 * b + y0 // 2) * 4 + 2 * (y0 % 2) + c) * 2 + h))
    left_far = lax.ppermute(left, ("y", "zl", "zh"), pairs)
    factor_g = lax.ppermute(factor_g, ("y", "zl", "zh"), moves)
    qg, qa, factor_g = lax.optimization_barrier((qg, qa, factor_g))
    result = call(
        finish_kernel,
        [((160, 640), BF16)],
        (
            *(left, swap(left), left_far, swap(left_far)),
            qg,
            qa,
            lax.dynamic_slice_in_dim(eig_a, block_a, 1, 0),
            lax.dynamic_slice_in_dim(eig_g, block_g, 1, 0).reshape(640, 1),
        ),
        10**9,
        3 * 10**6,
    )
    result = lax.ppermute(result, ("y", "zl", "zh"), moves)
    return factor_a, factor_g, result.T[None]


def solution(mesh):
    names = ("x", "y", "zl", "zh", "core")
    fine = Mesh(mesh.devices.reshape(4, 4, 4, 2, 2), names)
    dp, grp = names[:3], names[3:]
    return jax.shard_map(
        body,
        mesh=fine,
        in_specs=(
            P(names, None),
            P(names, None),
            P(None, grp, None),
            P(None, grp, None),
            P(),
            P(),
        ),
        out_specs=(P(names, None), P(names, None), P(dp, None, grp)),
        check_vma=False,
    )
```

profile of v0, /device:TPU:50, one launch (start us, length us, event | category | flops | bytes accessed | tf_op | source)
XLA Modules:
  0.0 168.9 jit_solution(420380947657630281)
XLA Ops:
  0.7 2.3 %constant_dynamic-slice_fusion.11 = (bf16[128,1280]{1,0:T(8,128)(2,1)S(1)}, bf16[128,1280]{1,0:T(8,128)(2,1)}, bf16[128,1280]{1,0:T(8,128)(2,1)S(1)}, bf16[128,1280]{1,0:T(8,128)(2,1)}) fusion(bf16[128,5120]{1,0:T(8,128)(2,1)} %param.7, s32[]{:T(128)S(6)} %select_n.760, s32[]{:T(128)S(6)} %select_n.761, s32[]{:T(128)S(6)} %select_n.763, s32[]{:T(128)S(6)} %select_n.762), kind=kLoop, calls=%fused_computation.21 | loop fusion | bytes 2621456 | tf_op jit(solution)/shard_map/dynamic_slice | solution.py:48
  3.0 1.3 collective-permute-start.5
  4.3 0.6 collective-permute-start.6
  4.9 1.1 collective-permute-start.7
  6.0 1.0 constant_dynamic-slice_fusion.15
  7.0 1.5 collective-permute-start
  8.5 1.1 collective-permute-start.1
  9.6 1.3 constant_dynamic-slice_fusion.6
  10.9 8.9 %collective-permute-done.5 = bf16[128,1280]{1,0:T(8,128)(2,1)} collective-permute-done((bf16[128,1280]{1,0:T(8,128)(2,1)}, bf16[128,1280]{1,0:T(8,128)(2,1)}, u32[]{:S(2)}, u32[]{:S(2)}) %collective-permute-start.5) | collective-permute-done | bytes 327712 | tf_op jit(solution)/shard_map/ppermute | solution.py:49
  19.8 0.5 collective-permute-start.2
  20.3 0.8 pad_maximum_fusion.4
  21.1 0.5 collective-permute-done.7
  21.6 1.3 pad_maximum_fusion.1.refs_3_
  22.9 1.6 collective-permute-start.8
  24.4 0.9 collective-permute-start.9
  25.3 3.3 %collective-permute-done.2 = bf16[128,1280]{1,0:T(8,128)(2,1)S(1)} collective-permute-done((bf16[128,1280]{1,0:T(8,128)(2,1)}, bf16[128,1280]{1,0:T(8,128)(2,1)S(1)}, u32[]{:S(2)}, u32[]{:S(2)}) %collective-permute-start.2) | collective-permute-done | bytes 327712 | tf_op jit(solution)/shard_map/ppermute | solution.py:49
  28.6 1.2 pad_maximum_fusion.refs_0_
  29.9 2.0 %collective-permute-start.4 = (bf16[512,1280]{1,0:T(8,128)(2,1)S(1)}, bf16[512,1280]{1,0:T(8,128)(2,1)}, u32[]{:S(2)}, u32[]{:S(2)}) collective-permute-start(bf16[512,1280]{1,0:T(8,128)(2,1)S(1)} %pad_maximum_fusion.refs_0_), channel_id=1, source_target_pairs={{0,48},{16,0},{32,16},{48,32},{1,49},{17,1},{33,17},{49,33},{2,50}... | collective-permute-start | bytes 3932168 | tf_op jit(solution)/shard_map/ppermute | solution.py:54
  32.0 6.4 %collective-permute-start.10 = (bf16[2,160,640]{2,1,0:T(8,128)(2,1)}, bf16[2,160,640]{2,1,0:T(8,128)(2,1)}, u32[]{:S(2)}, u32[]{:S(2)}) collective-permute-start(bf16[2,160,640]{2,1,0:T(8,128)(2,1)} %pad_maximum_fusion.4), channel_id=1, source_target_pairs={{0,2},{2,0},{1,3},{3,1},{4,6},{6,4},{5,7},{7,5},{8,10},{10,8},{9,1... | collective-permute-start | bytes 1228808 | tf_op jit(solution)/shard_map/ppermute | solution.py:36
  38.5 13.9 %collective-permute-done.8.refs_4_ = bf16[512,1280]{1,0:T(8,128)(2,1)} collective-permute-done((bf16[512,1280]{1,0:T(8,128)(2,1)S(1)}, bf16[512,1280]{1,0:T(8,128)(2,1)}, u32[]{:S(2)}, u32[]{:S(2)}) %collective-permute-start.8) | collective-permute-done | bytes 1310752 | tf_op jit(solution)/shard_map/ppermute | solution.py:54
  52.4 1.1 slice.26
  53.5 1.6 collective-permute-start.13
  55.1 0.1 collective-permute-done.9.refs_5_
  55.3 1.1 slice.27
  56.4 0.8 collective-permute-start.14
  57.2 1.2 collective-permute-done.3.refs_1_
  58.3 1.1 slice.24
  59.5 1.2 collective-permute-start.11
  60.7 1.1 slice.25
  61.8 1.2 collective-permute-start.12
  63.0 0.3 fusion.order_ref
  63.3 8.8 %shard_map.85 = (f32[2,640,1280]{2,1,0:T(8,128)S(1)}, f32[896,640]{1,0:T(8,128)S(1)}, bf16[384,1280]{1,0:T(8,128)(2,1)S(1)}, bf16[384,1280]{1,0:T(8,128)(2,1)S(1)}) custom-call(s32[5]{0:T(128)S(1)} %stack.69.where_ref, bf16[512,1280]{1,0:T(8,128)(2,1)S(1)} %pad_maximum_fusion.refs_0_, bf16[512,1280]{1,0:T(8,128)(2,1)} %collective-permute-done.3.refs_1_, ...), custom_call_target="tpu_custom_call" | custom-call | flops 5000000000 | bytes 10000000 | tf_op jit(solution)/shard_map/pallas_call | solution.py:211
  72.1 3.3 %collective-permute-done.11.al = bf16[256,1280]{1,0:T(8,128)(2,1)S(1)} collective-permute-done((bf16[256,1280]{1,0:T(8,128)(2,1)S(1)}, bf16[256,1280]{1,0:T(8,128)(2,1)S(1)}, u32[]{:S(2)}, u32[]{:S(2)}) %collective-permute-start.11) | collective-permute-done | bytes 655392 | tf_op jit(solution)/shard_map/ppermute | solution.py:61
  75.4 4.3 %collective-permute-done.12.ah = bf16[256,1280]{1,0:T(8,128)(2,1)S(1)} collective-permute-done((bf16[256,1280]{1,0:T(8,128)(2,1)S(1)}, bf16[256,1280]{1,0:T(8,128)(2,1)S(1)}, u32[]{:S(2)}, u32[]{:S(2)}) %collective-permute-start.12) | collective-permute-done | bytes 655392 | tf_op jit(solution)/shard_map/ppermute | solution.py:62
  79.7 8.3 %shard_map.86 = (bf16[8,208,640]{2,1,0:T(8,128)(2,1)S(1)}, bf16[8,208,640]{2,1,0:T(8,128)(2,1)S(1)}) custom-call(s32[5]{0:T(128)S(1)} %stack.69.where_ref, bf16[384,1280]{1,0:T(8,128)(2,1)S(1)} %get-tuple-element.44.acts_mid, bf16[384,1280]{1,0:T(8,128)(2,1)S(1)} %get-tuple-element.45.grads_mid, bf16[256,1280]{1,0:T(8,128)(2,1)S(1)} %collective-permute-done.11.al, ...), custom_call_target="tpu_custom_call" | custom-call | flops 4000000000 | bytes 10000000 | tf_op jit(solution)/shard_map/pallas_call | solution.py:211
  87.9 0.3 collective-permute-start.15
  88.3 4.1 %collective-permute-done.15.came = bf16[8,208,640]{2,1,0:T(8,128)(2,1)S(1)} collective-permute-done((bf16[8,208,640]{2,1,0:T(8,128)(2,1)S(1)}, bf16[8,208,640]{2,1,0:T(8,128)(2,1)S(1)}, u32[]{:S(2)}, u32[]{:S(2)}) %collective-permute-start.15) | collective-permute-done | bytes 2129952 | tf_op jit(solution)/shard_map/ppermute | solution.py:36
  92.4 0.5 shard_map.87
  92.9 2.3 %fusion.2 = (bf16[2,1,2,160,640]{4,3,2,0,1:T(8,128)(2,1)}, bf16[2,2,160,640]{3,2,1,0:T(8,128)(2,1)}) fusion(bf16[1,2,160,640]{3,2,1,0:T(8,128)(2,1)} %bitcast.6, bf16[1,2,160,640]{3,2,1,0:T(8,128)(2,1)S(1)} %maximum_bitcast_fusion), kind=kLoop, calls=%fused_computation.47 | loop fusion | flops 409600 | bytes 2457600 | tf_op jit(solution)/shard_map/stack | solution.py:285
  95.2 0.1 collective-permute-start.22
  95.4 1.9 %collective-permute-start.16 = (bf16[2,208,640]{2,1,0:T(8,128)(2,1)S(1)}, bf16[2,208,640]{2,1,0:T(8,128)(2,1)S(1)}, u32[]{:S(2)}, u32[]{:S(2)}) collective-permute-start(bf16[2,208,640]{2,1,0:T(8,128)(2,1)S(1)} %get-tuple-element.54), channel_id=1, source_target_pairs={{0,4},{4,8},{8,12},{12,2},{2,6},{6,10},{10,14},{14,0},{1,5},{5,9},... | collective-permute-start | bytes 1597448 | tf_op jit(solution)/shard_map/ppermute | solution.py:32
  97.3 0.1 collective-permute-start.17
  97.4 5.4 %collective-permute-start.19 = (bf16[112,640]{1,0:T(8,128)(2,1)S(1)}, bf16[112,640]{1,0:T(8,128)(2,1)S(1)}, u32[]{:S(2)}, u32[]{:S(2)}) collective-permute-start(bf16[112,640]{1,0:T(8,128)(2,1)S(1)} %get-tuple-element.59), channel_id=1, source_target_pairs={{0,10},{4,14},{8,0},{12,4},{2,8},{6,12},{10,2},{14,6},{1,11},{5,15... | collective-permute-start | bytes 430088 | tf_op jit(solution)/shard_map/ppermute | solution.py:32
  102.8 15.9 %collective-permute-done.18.up = bf16[96,640]{1,0:T(8,128)(2,1)S(1)} collective-permute-done((bf16[96,640]{1,0:T(8,128)(2,1)S(1)}, bf16[96,640]{1,0:T(8,128)(2,1)S(1)}, u32[]{:S(2)}, u32[]{:S(2)}) %collective-permute-start.18) | collective-permute-done | bytes 122912 | tf_op jit(solution)/shard_map/ppermute | solution.py:32
  118.7 0.2 shard_map.88
  118.9 2.4 %collective-permute-start.20 = (bf16[208,640]{1,0:T(8,128)(2,1)S(1)}, bf16[208,640]{1,0:T(8,128)(2,1)S(1)}, u32[]{:S(2)}, u32[]{:S(2)}) collective-permute-start(bf16[208,640]{1,0:T(8,128)(2,1)S(1)} %get-tuple-element.60), channel_id=1, source_target_pairs={{0,8},{4,12},{8,2},{12,6},{2,10},{6,14},{10,0},{14,4},{1,9},{5,13}... | collective-permute-start | bytes 798728 | tf_op jit(solution)/shard_map/ppermute | solution.py:32
  121.3 1.8 %collective-permute-start.21 = (bf16[208,640]{1,0:T(8,128)(2,1)S(1)}, bf16[208,640]{1,0:T(8,128)(2,1)S(1)}, u32[]{:S(2)}, u32[]{:S(2)}) collective-permute-start(bf16[208,640]{1,0:T(8,128)(2,1)S(1)} %get-tuple-element.61), channel_id=1, source_target_pairs={{0,10},{4,14},{8,0},{12,4},{2,8},{6,12},{10,2},{14,6},{1,11},{5,15... | collective-permute-start | bytes 798728 | tf_op jit(solution)/shard_map/ppermute | solution.py:32
  123.1 1.7 %maximum_select_fusion = bf16[2,2,2,160,640]{4,3,2,0,1:T(8,128)(2,1)S(1)} fusion(bf16[2,1,2,160,640]{4,3,2,0,1:T(8,128)(2,1)} %bitcast.8, bf16[2,1,2,160,640]{4,3,2,0,1:T(8,128)(2,1)S(1)} %copy-done.1, pred[]{:T(512)S(6)} %eq.420), kind=kLoop, calls=%fused_computation.3 | loop fusion | flops 2457600 | bytes 3276801 | tf_op jit(solution)/shard_map/jit(_where)/select_n | solution.py:285
  124.8 0.3 reverse_select_fusion
  125.2 0.1 fusion.3
  125.4 4.9 %collective-permute-done.20.ahead = bf16[208,640]{1,0:T(8,128)(2,1)S(1)} collective-permute-done((bf16[208,640]{1,0:T(8,128)(2,1)S(1)}, bf16[208,640]{1,0:T(8,128)(2,1)S(1)}, u32[]{:S(2)}, u32[]{:S(2)}) %collective-permute-start.20) | collective-permute-done | bytes 266272 | tf_op jit(solution)/shard_map/ppermute | solution.py:32
  130.3 1.0 shard_map.89
  131.2 7.4 %collective-permute-start.25 = (bf16[160,640]{1,0:T(8,128)(2,1)S(1)}, bf16[160,640]{1,0:T(8,128)(2,1)S(1)}, u32[]{:S(2)}, u32[]{:S(2)}) collective-permute-start(bf16[160,640]{1,0:T(8,128)(2,1)S(1)} %get-tuple-element.66.l0), channel_id=1, source_target_pairs={{0,14},{14,0},{4,8},{8,4},{12,2},{2,12},{10,6},{6,10},{24,20},{20,... | collective-permute-start | bytes 614408 | tf_op jit(solution)/shard_map/ppermute | solution.py:315
  138.6 0.2 copy.13.eig_g_ref
  138.8 0.7 constant_dynamic-slice_fusion.1.eig_a_ref
  139.6 1.9 %collective-permute-start.23 = (f32[20,640]{1,0:T(8,128)S(1)}, f32[20,640]{1,0:T(8,128)S(1)}, u32[]{:S(2)}, u32[]{:S(2)}) collective-permute-start(f32[20,640]{1,0:T(8,128)S(1)} %get-tuple-element.64), channel_id=1, source_target_pairs={{0,0},{14,2},{4,4},{8,6},{12,32},{2,34},{10,36},{6,38},{24,8},{20,... | collective-permute-start | bytes 153608 | tf_op jit(solution)/shard_map/ppermute | solution.py:316
  141.6 2.0 %collective-permute-done.25.l2 = bf16[160,640]{1,0:T(8,128)(2,1)S(1)} collective-permute-done((bf16[160,640]{1,0:T(8,128)(2,1)S(1)}, bf16[160,640]{1,0:T(8,128)(2,1)S(1)}, u32[]{:S(2)}, u32[]{:S(2)}) %collective-permute-start.25) | collective-permute-done | bytes 204832 | tf_op jit(solution)/shard_map/ppermute | solution.py:315
  143.6 0.1 pad_maximum_fusion.3.qg_ref
  143.7 7.6 %collective-permute-done.23 = f32[20,640]{1,0:T(8,128)S(1)} collective-permute-done((f32[20,640]{1,0:T(8,128)S(1)}, f32[20,640]{1,0:T(8,128)S(1)}, u32[]{:S(2)}, u32[]{:S(2)}) %collective-permute-start.23) | collective-permute-done | bytes 51232 | tf_op jit(solution)/shard_map/ppermute | solution.py:316
  151.4 2.2 %shard_map.90 = bf16[160,640]{1,0:T(8,128)(2,1)S(1)} custom-call(bf16[160,640]{1,0:T(8,128)(2,1)S(1)} %get-tuple-element.66.l0, bf16[160,640]{1,0:T(8,128)(2,1)S(1)} %collective-permute-done.24.l1, bf16[160,640]{1,0:T(8,128)(2,1)S(1)} %collective-permute-done.25.l2, bf16[160,640]{1,0:T(8,128)(2,1)S(1)} %collective-permute-done.26.l3, ...), custom_call_target="tpu_custom_call" | custom-call | flops 1000000000 | bytes 3000000 | tf_op jit(solution)/shard_map/pallas_call | solution.py:211
  153.6 1.9 %collective-permute-start.27 = (bf16[160,640]{1,0:T(8,128)(2,1)S(1)}, bf16[160,640]{1,0:T(8,128)(2,1)S(1)}, u32[]{:S(2)}, u32[]{:S(2)}) collective-permute-start(bf16[160,640]{1,0:T(8,128)(2,1)S(1)} %shard_map.90), channel_id=1, source_target_pairs={{0,0},{14,2},{4,4},{8,6},{12,32},{2,34},{10,36},{6,38},{24,8},{20,... | collective-permute-start | bytes 614408 | tf_op jit(solution)/shard_map/ppermute | solution.py:331
  155.5 12.1 %collective-permute-done.27 = bf16[160,640]{1,0:T(8,128)(2,1)S(1)} collective-permute-done((bf16[160,640]{1,0:T(8,128)(2,1)S(1)}, bf16[160,640]{1,0:T(8,128)(2,1)S(1)}, u32[]{:S(2)}, u32[]{:S(2)}) %collective-permute-start.27) | collective-permute-done | bytes 204832 | tf_op jit(solution)/shard_map/ppermute | solution.py:331
  167.6 0.6 copy.16
  168.2 0.7 copy.17
  (39 shorter events, 0.7 us)
Async XLA Ops:
  0.6 138.0 %copy-start = (f32[8,640]{1,0:T(8,128)S(1)}, f32[8,640]{1,0:T(8,128)}, u32[]{:S(2)}) copy-start(f32[8,640]{1,0:T(8,128)} %param.11) | copy-start | bytes 61444
  0.6 5.3 %copy-start.2 = (bf16[128,5120]{1,0:T(8,128)(2,1)S(1)}, bf16[128,5120]{1,0:T(8,128)(2,1)}, u32[]{:S(2)}) copy-start(bf16[128,5120]{1,0:T(8,128)(2,1)} %param.6) | copy-start | bytes 3932164
  3.0 16.8 %collective-permute-start.5 = (bf16[128,1280]{1,0:T(8,128)(2,1)}, bf16[128,1280]{1,0:T(8,128)(2,1)}, u32[]{:S(2)}, u32[]{:S(2)}) collective-permute-start(bf16[128,1280]{1,0:T(8,128)(2,1)} %get-tuple-element.76), channel_id=1, source_target_pairs={{0,16},{16,32},{32,48},{48,0},{1,17},{17,33},{33,49},{49,1},{2,18}... | collective-permute-start | bytes 983048 | tf_op jit(solution)/shard_map/ppermute | solution.py:49
  4.3 16.8 %collective-permute-start.6 = (bf16[128,1280]{1,0:T(8,128)(2,1)}, bf16[128,1280]{1,0:T(8,128)(2,1)}, u32[]{:S(2)}, u32[]{:S(2)}) collective-permute-start(bf16[128,1280]{1,0:T(8,128)(2,1)} %get-tuple-element.78), channel_id=1, source_target_pairs={{0,32},{16,48},{32,0},{48,16},{1,33},{17,49},{33,1},{49,17},{2,34}... | collective-permute-start | bytes 983048 | tf_op jit(solution)/shard_map/ppermute | solution.py:49
  4.9 16.7 %collective-permute-start.7 = (bf16[128,1280]{1,0:T(8,128)(2,1)S(1)}, bf16[128,1280]{1,0:T(8,128)(2,1)}, u32[]{:S(2)}, u32[]{:S(2)}) collective-permute-start(bf16[128,1280]{1,0:T(8,128)(2,1)S(1)} %get-tuple-element.77), channel_id=1, source_target_pairs={{0,48},{16,0},{32,16},{48,32},{1,49},{17,1},{33,17},{49,33},{2,50}... | collective-permute-start | bytes 983048 | tf_op jit(solution)/shard_map/ppermute | solution.py:49
  7.0 18.3 %collective-permute-start = (bf16[128,1280]{1,0:T(8,128)(2,1)}, bf16[128,1280]{1,0:T(8,128)(2,1)}, u32[]{:S(2)}, u32[]{:S(2)}) collective-permute-start(bf16[128,1280]{1,0:T(8,128)(2,1)} %get-tuple-element.80), channel_id=1, source_target_pairs={{0,64},{64,128},{128,192},{192,0},{1,65},{65,129},{129,193},{193,1... | collective-permute-start | bytes 983048 | tf_op jit(solution)/shard_map/ppermute | solution.py:49
  8.5 16.9 %collective-permute-start.1 = (bf16[128,1280]{1,0:T(8,128)(2,1)}, bf16[128,1280]{1,0:T(8,128)(2,1)}, u32[]{:S(2)}, u32[]{:S(2)}) collective-permute-start(bf16[128,1280]{1,0:T(8,128)(2,1)} %get-tuple-element.82), channel_id=1, source_target_pairs={{0,128},{64,192},{128,0},{192,64},{1,129},{65,193},{129,1},{193,65... | collective-permute-start | bytes 983048 | tf_op jit(solution)/shard_map/ppermute | solution.py:49
  19.8 8.8 %collective-permute-start.2 = (bf16[128,1280]{1,0:T(8,128)(2,1)}, bf16[128,1280]{1,0:T(8,128)(2,1)S(1)}, u32[]{:S(2)}, u32[]{:S(2)}) collective-permute-start(bf16[128,1280]{1,0:T(8,128)(2,1)} %get-tuple-element.81), channel_id=1, source_target_pairs={{0,192},{64,0},{128,64},{192,128},{1,193},{65,1},{129,65},{193,129... | collective-permute-start | bytes 983048 | tf_op jit(solution)/shard_map/ppermute | solution.py:49
  22.9 29.5 %collective-permute-start.8 = (bf16[512,1280]{1,0:T(8,128)(2,1)S(1)}, bf16[512,1280]{1,0:T(8,128)(2,1)}, u32[]{:S(2)}, u32[]{:S(2)}) collective-permute-start(bf16[512,1280]{1,0:T(8,128)(2,1)S(1)} %pad_maximum_fusion.1.refs_3_), channel_id=1, source_target_pairs={{0,64},{64,128},{128,192},{192,0},{1,65},{65,129},{129,193},{193,1... | collective-permute-start | bytes 3932168 | tf_op jit(solution)/shard_map/ppermute | solution.py:54
  24.4 30.8 %collective-permute-start.9 = (bf16[512,1280]{1,0:T(8,128)(2,1)S(1)}, bf16[512,1280]{1,0:T(8,128)(2,1)}, u32[]{:S(2)}, u32[]{:S(2)}) collective-permute-start(bf16[512,1280]{1,0:T(8,128)(2,1)S(1)} %pad_maximum_fusion.1.refs_3_), channel_id=1, source_target_pairs={{0,192},{64,0},{128,64},{192,128},{1,193},{65,1},{129,65},{193,129... | collective-permute-start | bytes 3932168 | tf_op jit(solution)/shard_map/ppermute | solution.py:54
  29.8 28.6 %collective-permute-start.3 = (bf16[512,1280]{1,0:T(8,128)(2,1)S(1)}, bf16[512,1280]{1,0:T(8,128)(2,1)}, u32[]{:S(2)}, u32[]{:S(2)}) collective-permute-start(bf16[512,1280]{1,0:T(8,128)(2,1)S(1)} %pad_maximum_fusion.refs_0_), channel_id=1, source_target_pairs={{0,16},{16,32},{32,48},{48,0},{1,17},{17,33},{33,49},{49,1},{2,18}... | collective-permute-start | bytes 3932168 | tf_op jit(solution)/shard_map/ppermute | solution.py:54
  29.9 30.8 %collective-permute-start.4 = (bf16[512,1280]{1,0:T(8,128)(2,1)S(1)}, bf16[512,1280]{1,0:T(8,128)(2,1)}, u32[]{:S(2)}, u32[]{:S(2)}) collective-permute-start(bf16[512,1280]{1,0:T(8,128)(2,1)S(1)} %pad_maximum_fusion.refs_0_), channel_id=1, source_target_pairs={{0,48},{16,0},{32,16},{48,32},{1,49},{17,1},{33,17},{49,33},{2,50}... | collective-permute-start | bytes 3932168 | tf_op jit(solution)/shard_map/ppermute | solution.py:54
  32.0 31.3 %collective-permute-start.10 = (bf16[2,160,640]{2,1,0:T(8,128)(2,1)}, bf16[2,160,640]{2,1,0:T(8,128)(2,1)}, u32[]{:S(2)}, u32[]{:S(2)}) collective-permute-start(bf16[2,160,640]{2,1,0:T(8,128)(2,1)} %pad_maximum_fusion.4), channel_id=1, source_target_pairs={{0,2},{2,0},{1,3},{3,1},{4,6},{6,4},{5,7},{7,5},{8,10},{10,8},{9,1... | collective-permute-start | bytes 1228808 | tf_op jit(solution)/shard_map/ppermute | solution.py:36
  53.5 18.5 %collective-permute-start.13 = (bf16[256,1280]{1,0:T(8,128)(2,1)S(1)}, bf16[256,1280]{1,0:T(8,128)(2,1)S(1)}, u32[]{:S(2)}, u32[]{:S(2)}) collective-permute-start(bf16[256,1280]{1,0:T(8,128)(2,1)S(1)} %slice.26), channel_id=1, source_target_pairs={{0,64},{64,128},{128,192},{192,0},{1,65},{65,129},{129,193},{193,1... | collective-permute-start | bytes 1966088 | tf_op jit(solution)/shard_map/ppermute | solution.py:61
  56.4 15.7 %collective-permute-start.14 = (bf16[256,1280]{1,0:T(8,128)(2,1)S(1)}, bf16[256,1280]{1,0:T(8,128)(2,1)S(1)}, u32[]{:S(2)}, u32[]{:S(2)}) collective-permute-start(bf16[256,1280]{1,0:T(8,128)(2,1)S(1)} %slice.27), channel_id=1, source_target_pairs={{0,192},{64,0},{128,64},{192,128},{1,193},{65,1},{129,65},{193,129... | collective-permute-start | bytes 1966088 | tf_op jit(solution)/shard_map/ppermute | solution.py:62
  59.5 15.9 %collective-permute-start.11 = (bf16[256,1280]{1,0:T(8,128)(2,1)S(1)}, bf16[256,1280]{1,0:T(8,128)(2,1)S(1)}, u32[]{:S(2)}, u32[]{:S(2)}) collective-permute-start(bf16[256,1280]{1,0:T(8,128)(2,1)S(1)} %slice.24), channel_id=1, source_target_pairs={{0,16},{16,32},{32,48},{48,0},{1,17},{17,33},{33,49},{49,1},{2,18}... | collective-permute-start | bytes 1966088 | tf_op jit(solution)/shard_map/ppermute | solution.py:61
  61.8 17.9 %collective-permute-start.12 = (bf16[256,1280]{1,0:T(8,128)(2,1)S(1)}, bf16[256,1280]{1,0:T(8,128)(2,1)S(1)}, u32[]{:S(2)}, u32[]{:S(2)}) collective-permute-start(bf16[256,1280]{1,0:T(8,128)(2,1)S(1)} %slice.25), channel_id=1, source_target_pairs={{0,48},{16,0},{32,16},{48,32},{1,49},{17,1},{33,17},{49,33},{2,50}... | collective-permute-start | bytes 1966088 | tf_op jit(solution)/shard_map/ppermute | solution.py:62
  87.9 4.5 %collective-permute-start.15 = (bf16[8,208,640]{2,1,0:T(8,128)(2,1)S(1)}, bf16[8,208,640]{2,1,0:T(8,128)(2,1)S(1)}, u32[]{:S(2)}, u32[]{:S(2)}) collective-permute-start(bf16[8,208,640]{2,1,0:T(8,128)(2,1)S(1)} %get-tuple-element.50), channel_id=1, source_target_pairs={{0,1},{1,0},{2,3},{3,2},{4,5},{5,4},{6,7},{7,6},{8,9},{9,8},{10,11... | collective-permute-start | bytes 6389768 | tf_op jit(solution)/shard_map/ppermute | solution.py:36
  95.2 27.9 %collective-permute-start.22 = (bf16[2,2,160,640]{3,2,1,0:T(8,128)(2,1)}, bf16[2,2,160,640]{3,2,1,0:T(8,128)(2,1)}, u32[]{:S(2)}, u32[]{:S(2)}) collective-permute-start(bf16[2,2,160,640]{3,2,1,0:T(8,128)(2,1)} %get-tuple-element.88), channel_id=1, source_target_pairs={{0,1},{1,0},{2,3},{3,2},{4,5},{5,4},{6,7},{7,6},{8,9},{9,8},{10,11... | collective-permute-start | bytes 2457608 | tf_op jit(solution)/shard_map/ppermute | solution.py:36
  95.4 23.3 %collective-permute-start.16 = (bf16[2,208,640]{2,1,0:T(8,128)(2,1)S(1)}, bf16[2,208,640]{2,1,0:T(8,128)(2,1)S(1)}, u32[]{:S(2)}, u32[]{:S(2)}) collective-permute-start(bf16[2,208,640]{2,1,0:T(8,128)(2,1)S(1)} %get-tuple-element.54), channel_id=1, source_target_pairs={{0,4},{4,8},{8,12},{12,2},{2,6},{6,10},{10,14},{14,0},{1,5},{5,9},... | collective-permute-start | bytes 1597448 | tf_op jit(solution)/shard_map/ppermute | solution.py:32
  97.3 21.4 %collective-permute-start.17 = (bf16[2,208,640]{2,1,0:T(8,128)(2,1)S(1)}, bf16[2,208,640]{2,1,0:T(8,128)(2,1)S(1)}, u32[]{:S(2)}, u32[]{:S(2)}) collective-permute-start(bf16[2,208,640]{2,1,0:T(8,128)(2,1)S(1)} %get-tuple-element.55), channel_id=1, source_target_pairs={{0,14},{4,0},{8,4},{12,8},{2,12},{6,2},{10,6},{14,10},{1,15},{5,1}... | collective-permute-start | bytes 1597448 | tf_op jit(solution)/shard_map/ppermute | solution.py:32
  97.4 21.3 %collective-permute-start.19 = (bf16[112,640]{1,0:T(8,128)(2,1)S(1)}, bf16[112,640]{1,0:T(8,128)(2,1)S(1)}, u32[]{:S(2)}, u32[]{:S(2)}) collective-permute-start(bf16[112,640]{1,0:T(8,128)(2,1)S(1)} %get-tuple-element.59), channel_id=1, source_target_pairs={{0,10},{4,14},{8,0},{12,4},{2,8},{6,12},{10,2},{14,6},{1,11},{5,15... | collective-permute-start | bytes 430088 | tf_op jit(solution)/shard_map/ppermute | solution.py:32
  102.8 15.9 %collective-permute-start.18 = (bf16[96,640]{1,0:T(8,128)(2,1)S(1)}, bf16[96,640]{1,0:T(8,128)(2,1)S(1)}, u32[]{:S(2)}, u32[]{:S(2)}) collective-permute-start(bf16[96,640]{1,0:T(8,128)(2,1)S(1)} %get-tuple-element.58), channel_id=1, source_target_pairs={{0,8},{4,12},{8,2},{12,6},{2,10},{6,14},{10,0},{14,4},{1,9},{5,13}... | collective-permute-start | bytes 368648 | tf_op jit(solution)/shard_map/ppermute | solution.py:32
  102.8 20.3 %copy-start.1 = (bf16[2,1,2,160,640]{4,3,2,0,1:T(8,128)(2,1)S(1)}, bf16[2,1,2,160,640]{4,3,2,0,1:T(8,128)(2,1)}, u32[]{:S(2)}) copy-start(bf16[2,1,2,160,640]{4,3,2,0,1:T(8,128)(2,1)} %get-tuple-element.87) | copy-start | bytes 2457604
  118.9 11.4 %collective-permute-start.20 = (bf16[208,640]{1,0:T(8,128)(2,1)S(1)}, bf16[208,640]{1,0:T(8,128)(2,1)S(1)}, u32[]{:S(2)}, u32[]{:S(2)}) collective-permute-start(bf16[208,640]{1,0:T(8,128)(2,1)S(1)} %get-tuple-element.60), channel_id=1, source_target_pairs={{0,8},{4,12},{8,2},{12,6},{2,10},{6,14},{10,0},{14,4},{1,9},{5,13}... | collective-permute-start | bytes 798728 | tf_op jit(solution)/shard_map/ppermute | solution.py:32
  121.3 9.0 %collective-permute-start.21 = (bf16[208,640]{1,0:T(8,128)(2,1)S(1)}, bf16[208,640]{1,0:T(8,128)(2,1)S(1)}, u32[]{:S(2)}, u32[]{:S(2)}) collective-permute-start(bf16[208,640]{1,0:T(8,128)(2,1)S(1)} %get-tuple-element.61), channel_id=1, source_target_pairs={{0,10},{4,14},{8,0},{12,4},{2,8},{6,12},{10,2},{14,6},{1,11},{5,15... | collective-permute-start | bytes 798728 | tf_op jit(solution)/shard_map/ppermute | solution.py:32
  131.2 12.3 %collective-permute-start.25 = (bf16[160,640]{1,0:T(8,128)(2,1)S(1)}, bf16[160,640]{1,0:T(8,128)(2,1)S(1)}, u32[]{:S(2)}, u32[]{:S(2)}) collective-permute-start(bf16[160,640]{1,0:T(8,128)(2,1)S(1)} %get-tuple-element.66.l0), channel_id=1, source_target_pairs={{0,14},{14,0},{4,8},{8,4},{12,2},{2,12},{10,6},{6,10},{24,20},{20,... | collective-permute-start | bytes 614408 | tf_op jit(solution)/shard_map/ppermute | solution.py:315
  139.6 11.8 %collective-permute-start.24 = (bf16[160,640]{1,0:T(8,128)(2,1)S(1)}, bf16[160,640]{1,0:T(8,128)(2,1)S(1)}, u32[]{:S(2)}, u32[]{:S(2)}) collective-permute-start(bf16[160,640]{1,0:T(8,128)(2,1)S(1)} %get-tuple-element.66.l0), channel_id=1, source_target_pairs={{0,1},{1,0},{2,3},{3,2},{4,5},{5,4},{6,7},{7,6},{8,9},{9,8},{10,11... | collective-permute-start | bytes 614408 | tf_op jit(solution)/shard_map/ppermute | solution.py:36
  139.6 11.7 %collective-permute-start.23 = (f32[20,640]{1,0:T(8,128)S(1)}, f32[20,640]{1,0:T(8,128)S(1)}, u32[]{:S(2)}, u32[]{:S(2)}) collective-permute-start(f32[20,640]{1,0:T(8,128)S(1)} %get-tuple-element.64), channel_id=1, source_target_pairs={{0,0},{14,2},{4,4},{8,6},{12,32},{2,34},{10,36},{6,38},{24,8},{20,... | collective-permute-start | bytes 153608 | tf_op jit(solution)/shard_map/ppermute | solution.py:316
  143.5 7.8 %collective-permute-start.26 = (bf16[160,640]{1,0:T(8,128)(2,1)S(1)}, bf16[160,640]{1,0:T(8,128)(2,1)S(1)}, u32[]{:S(2)}, u32[]{:S(2)}) collective-permute-start(bf16[160,640]{1,0:T(8,128)(2,1)S(1)} %collective-permute-done.25.l2), channel_id=1, source_target_pairs={{0,1},{1,0},{2,3},{3,2},{4,5},{5,4},{6,7},{7,6},{8,9},{9,8},{10,11... | collective-permute-start | bytes 614408 | tf_op jit(solution)/shard_map/ppermute | solution.py:36
  153.6 14.0 %collective-permute-start.27 = (bf16[160,640]{1,0:T(8,128)(2,1)S(1)}, bf16[160,640]{1,0:T(8,128)(2,1)S(1)}, u32[]{:S(2)}, u32[]{:S(2)}) collective-permute-start(bf16[160,640]{1,0:T(8,128)(2,1)S(1)} %shard_map.90), channel_id=1, source_target_pairs={{0,0},{14,2},{4,4},{8,6},{12,32},{2,34},{10,36},{6,38},{24,8},{20,... | collective-permute-start | bytes 614408 | tf_op jit(solution)/shard_map/ppermute | solution.py:331
where the time goes:
time: 169 us
  waiting for transfers between devices  82 us (49%)
  starting transfers between devices  45 us (27%)
  Pallas kernels  20.9 us (12%)
  local copies, waits for them, and re-layouts  11.9 us (7%)
  other arithmetic  8.13 us (5%)
    pallas_call x6, Pallas kernels, call(): pl.pallas_call(kernel, out_shape=shapes, in_specs=([] if scalars is None...  20.9 us
    ppermute x6, waiting for transfers between devices, to_z(): return lax.ppermute(array, ('zl', 'zh'), z_shift(by))  20.7 us
    ppermute x2, waiting for transfers between devices, gather_near(): lax.ppermute(own, axis, shift(4, 1))  15 us
    ppermute x6, waiting for transfers between devices, exchange(): got[d] = cols if d == 0 else lax.ppermute(cols, axis, shift(count, d))  12.7 us
    ppermute x1, waiting for transfers between devices, body(): result = lax.ppermute(result, ('y', 'zl', 'zh'), moves)  12.1 us
    ppermute x6, starting transfers between devices, to_z(): return lax.ppermute(array, ('zl', 'zh'), z_shift(by))  11.7 us
    ppermute x1, waiting for transfers between devices, body(): factor_g = lax.ppermute(factor_g, ('y', 'zl', 'zh'), moves)  7.6 us
    ppermute x1, starting transfers between devices, body(): left_far = lax.ppermute(left, ('y', 'zl', 'zh'), pairs)  7.36 us
  transfers between devices with their start and end apart: 28, of which 14 were waited for; matrix products, arithmetic and copies ran while one was open for 8% of the time, Pallas kernels for 5%

commit v1 on v0

--- a/solution.py
+++ b/solution.py
@@ -244,7 +244,9 @@
         )
 
     acts_own, grads_own = exchange([(acts, "x"), (grads, "y")], 4, 1280)
-    basis_out, acts_own = lax.optimization_barrier((basis_pair(theirs), acts_own))
+    basis_out, basis_mine, acts_own = lax.optimization_barrier(
+        (basis_pair(theirs), basis_pair(mine), acts_own)
+    )
     basis_far = swap(basis_out, "zh")
     near = (*gather_near(acts_own, "y"), *gather_near(grads_own, "x"))
     acts_far, grads_far = gather_far(near[:3], "y"), gather_far(near[3:], "x")
@@ -278,24 +280,28 @@
         10**6,
         4 * 10**6,
     )
-    basis_far, to_next = lax.optimization_barrier((basis_far, to_next))
-
-    here = jnp.stack([basis_pair(mine), basis_far])
-    sibling = swap(here)
-    by_core = jnp.where(core == 0, jnp.stack([here, sibling], 1), jnp.stack([sibling, here], 1))
-    whole = jnp.where(zh == 0, by_core, by_core[::-1])
-    qa = whole[:, :, 0].reshape(4, 160, 640)
-    qg = whole[:, :, 1].reshape(4, 160, 640)
-    qg = jnp.stack(
-        [lax.dynamic_index_in_dim(qg, quarter ^ r, 0, keepdims=False) for r in range(4)]
-    )
-
     prev, after = to_z(to_next, 1), to_z(to_prev, 7)
     up, down = to_z(up, 2), to_z(down, 6)
     ahead, behind = call(
         parity_sum_kernel, [one, one], (two, six, prev, after, up, down), 10**6, 10**6
     )
+    ahead, basis_mine, basis_far = lax.optimization_barrier((ahead, basis_mine, basis_far))
     ahead, behind = to_z(ahead, 2), to_z(behind, 6)
+
+    def by_core(rows):
+        other = swap(rows)
+        return jnp.where(core == 0, jnp.stack([rows, other], 1), jnp.stack([other, rows], 1))
+
+    near_rows, far_rows = by_core(basis_mine), by_core(basis_far)
+    whole = jnp.where(
+        zh == 0,
+        jnp.concatenate([near_rows, far_rows], axis=1),
+        jnp.concatenate([far_rows, near_rows], axis=1),
+    )
+    qa = whole[0]
+    qg = jnp.stack(
+        [lax.dynamic_index_in_dim(whole[1], quarter ^ r, 0, keepdims=False) for r in range(4)]
+    )
     left, factor_a, factor_g = call(
         left_kernel,
         [((160, 640), BF16), ((20, 640), F32), ((20, 640), F32)],

time: 169 us -> 168 us (level)
    another operation x3 -> x1, other arithmetic: 2.49 us -> 0.13 us  [body(): jnp.stack([lax.dynamic_index_in_dim(whole[1], quarter ^ r, 0, keepdims=Fa...]
    ppermute x5 -> x6, starting transfers between devices: 6.83 us -> 7.28 us  [swap(): return lax.ppermute(array, axis, shift(2, 1))]
    ppermute x5 -> x6, waiting for transfers between devices: 4.15 us -> 4.21 us  [swap(): return lax.ppermute(array, axis, shift(2, 1))]
  transfers between devices with their start and end apart: 28 -> 29, of which waited for: 14 -> 15; matrix products, arithmetic and copies ran while one was open for 8% -> 9% of each run, Pallas kernels for 5% -> 5%
where the time goes in v1:
time: 168 us
  waiting for transfers between devices  80.4 us (48%)
  starting transfers between devices  45.8 us (27%)
  Pallas kernels  20.9 us (12%)
  local copies, waits for them, and re-layouts  12.9 us (8%)
  other arithmetic  6.52 us (4%)
    pallas_call x6, Pallas kernels, call(): pl.pallas_call(kernel, out_shape=shapes, in_specs=([] if scalars is None...  20.9 us
    ppermute x6, waiting for transfers between devices, to_z(): return lax.ppermute(array, ('zl', 'zh'), z_shift(by))  20.2 us
    ppermute x2, waiting for transfers between devices, gather_near(): lax.ppermute(own, axis, shift(4, 1))  15.2 us
    ppermute x1, waiting for transfers between devices, body(): result = lax.ppermute(result, ('y', 'zl', 'zh'), moves)  12.1 us
    ppermute x6, starting transfers between devices, to_z(): return lax.ppermute(array, ('zl', 'zh'), z_shift(by))  11.6 us
    ppermute x6, waiting for transfers between devices, exchange(): got[d] = cols if d == 0 else lax.ppermute(cols, axis, shift(count, d))  11.5 us
    ppermute x1, starting transfers between devices, body(): left_far = lax.ppermute(left, ('y', 'zl', 'zh'), pairs)  7.63 us
    ppermute x6, starting transfers between devices, swap(): return lax.ppermute(array, axis, shift(2, 1))  7.28 us
  transfers between devices with their start and end apart: 29, of which 15 were waited for; matrix products, arithmetic and copies ran while one was open for 9% of the time, Pallas kernels for 5%

profile of v1, /device:TPU:50, one launch (start us, length us, event | category | flops | bytes accessed | tf_op | source)
XLA Modules:
  0.0 167.5 jit_solution(8257073979512554979)
XLA Ops:
  0.7 2.4 %constant_dynamic-slice_fusion.5 = (bf16[128,1280]{1,0:T(8,128)(2,1)S(1)}, bf16[128,1280]{1,0:T(8,128)(2,1)}, bf16[128,1280]{1,0:T(8,128)(2,1)}, bf16[128,1280]{1,0:T(8,128)(2,1)}) fusion(bf16[128,5120]{1,0:T(8,128)(2,1)} %param.7, s32[]{:T(128)S(6)} %select_n.778, s32[]{:T(128)S(6)} %select_n.779, s32[]{:T(128)S(6)} %select_n.781, s32[]{:T(128)S(6)} %select_n.780), kind=kLoop, calls=%fused_computation.20 | loop fusion | bytes 2621456 | tf_op jit(solution)/shard_map/dynamic_slice | solution.py:48
  3.1 1.3 collective-permute-start.5
  4.4 0.6 collective-permute-start.6
  5.0 1.1 collective-permute-start.7
  6.0 1.0 constant_dynamic-slice_fusion.9
  7.1 1.5 collective-permute-start
  8.6 1.1 collective-permute-start.1
  9.7 1.1 constant_dynamic-slice_fusion.11
  10.8 1.1 constant_dynamic-slice_fusion.10
  11.8 7.9 %collective-permute-done.5 = bf16[128,1280]{1,0:T(8,128)(2,1)S(1)} collective-permute-done((bf16[128,1280]{1,0:T(8,128)(2,1)}, bf16[128,1280]{1,0:T(8,128)(2,1)S(1)}, u32[]{:S(2)}, u32[]{:S(2)}) %collective-permute-start.5) | collective-permute-done | bytes 327712 | tf_op jit(solution)/shard_map/ppermute | solution.py:49
  19.8 0.5 collective-permute-start.2
  20.3 0.2 copy-done.2
  20.5 0.9 pad_maximum_fusion.3
  21.4 0.3 collective-permute-done.7
  21.7 1.2 pad_maximum_fusion.1.refs_3_
  22.9 1.6 collective-permute-start.8
  24.4 0.9 collective-permute-start.9
  25.4 3.2 %collective-permute-done.2 = bf16[128,1280]{1,0:T(8,128)(2,1)S(1)} collective-permute-done((bf16[128,1280]{1,0:T(8,128)(2,1)}, bf16[128,1280]{1,0:T(8,128)(2,1)S(1)}, u32[]{:S(2)}, u32[]{:S(2)}) %collective-permute-start.2) | collective-permute-done | bytes 327712 | tf_op jit(solution)/shard_map/ppermute | solution.py:49
  28.6 1.2 pad_maximum_fusion.refs_0_
  29.8 2.0 %collective-permute-start.4 = (bf16[512,1280]{1,0:T(8,128)(2,1)S(1)}, bf16[512,1280]{1,0:T(8,128)(2,1)}, u32[]{:S(2)}, u32[]{:S(2)}) collective-permute-start(bf16[512,1280]{1,0:T(8,128)(2,1)S(1)} %pad_maximum_fusion.refs_0_), channel_id=1, source_target_pairs={{0,48},{16,0},{32,16},{48,32},{1,49},{17,1},{33,17},{49,33},{2,50}... | collective-permute-start | bytes 3932168 | tf_op jit(solution)/shard_map/ppermute | solution.py:54
  31.9 6.4 %collective-permute-start.10 = (bf16[2,160,640]{2,1,0:T(8,128)(2,1)}, bf16[2,160,640]{2,1,0:T(8,128)(2,1)S(1)}, u32[]{:S(2)}, u32[]{:S(2)}) collective-permute-start(bf16[2,160,640]{2,1,0:T(8,128)(2,1)} %get-tuple-element.39), channel_id=1, source_target_pairs={{0,2},{2,0},{1,3},{3,1},{4,6},{6,4},{5,7},{7,5},{8,10},{10,8},{9,1... | collective-permute-start | bytes 1228808 | tf_op jit(solution)/shard_map/ppermute | solution.py:36
  38.5 13.9 %collective-permute-done.8.refs_4_ = bf16[512,1280]{1,0:T(8,128)(2,1)} collective-permute-done((bf16[512,1280]{1,0:T(8,128)(2,1)S(1)}, bf16[512,1280]{1,0:T(8,128)(2,1)}, u32[]{:S(2)}, u32[]{:S(2)}) %collective-permute-start.8) | collective-permute-done | bytes 1310752 | tf_op jit(solution)/shard_map/ppermute | solution.py:54
  52.4 1.1 slice.29
  53.5 1.6 collective-permute-start.13
  55.2 1.1 slice.30
  56.4 0.8 collective-permute-start.14
  57.1 1.3 collective-permute-done.3.refs_1_
  58.5 1.1 slice.27
  59.6 1.2 collective-permute-start.11
  60.8 1.1 slice.28
  61.9 1.2 collective-permute-start.12
  63.1 0.3 fusion.order_ref
  63.4 8.8 %shard_map.85 = (f32[2,640,1280]{2,1,0:T(8,128)S(1)}, f32[896,640]{1,0:T(8,128)S(1)}, bf16[384,1280]{1,0:T(8,128)(2,1)S(1)}, bf16[384,1280]{1,0:T(8,128)(2,1)S(1)}) custom-call(s32[5]{0:T(128)S(1)} %stack.74.where_ref, bf16[512,1280]{1,0:T(8,128)(2,1)S(1)} %pad_maximum_fusion.refs_0_, bf16[512,1280]{1,0:T(8,128)(2,1)} %collective-permute-done.3.refs_1_, ...), custom_call_target="tpu_custom_call" | custom-call | flops 5000000000 | bytes 10000000 | tf_op jit(solution)/shard_map/pallas_call | solution.py:211
  72.2 3.3 %collective-permute-done.11.al = bf16[256,1280]{1,0:T(8,128)(2,1)S(1)} collective-permute-done((bf16[256,1280]{1,0:T(8,128)(2,1)S(1)}, bf16[256,1280]{1,0:T(8,128)(2,1)S(1)}, u32[]{:S(2)}, u32[]{:S(2)}) %collective-permute-start.11) | collective-permute-done | bytes 655392 | tf_op jit(solution)/shard_map/ppermute | solution.py:61
  75.5 4.3 %collective-permute-done.12.ah = bf16[256,1280]{1,0:T(8,128)(2,1)S(1)} collective-permute-done((bf16[256,1280]{1,0:T(8,128)(2,1)S(1)}, bf16[256,1280]{1,0:T(8,128)(2,1)S(1)}, u32[]{:S(2)}, u32[]{:S(2)}) %collective-permute-start.12) | collective-permute-done | bytes 655392 | tf_op jit(solution)/shard_map/ppermute | solution.py:62
  79.8 8.3 %shard_map.86 = (bf16[8,208,640]{2,1,0:T(8,128)(2,1)S(1)}, bf16[8,208,640]{2,1,0:T(8,128)(2,1)S(1)}) custom-call(s32[5]{0:T(128)S(1)} %stack.74.where_ref, bf16[384,1280]{1,0:T(8,128)(2,1)S(1)} %get-tuple-element.46.acts_mid, bf16[384,1280]{1,0:T(8,128)(2,1)S(1)} %get-tuple-element.47.grads_mid, bf16[256,1280]{1,0:T(8,128)(2,1)S(1)} %collective-permute-done.11.al, ...), custom_call_target="tpu_custom_call" | custom-call | flops 4000000000 | bytes 10000000 | tf_op jit(solution)/shard_map/pallas_call | solution.py:211
  88.0 0.3 collective-permute-start.15
  88.4 4.2 %collective-permute-done.15.came = bf16[8,208,640]{2,1,0:T(8,128)(2,1)S(1)} collective-permute-done((bf16[8,208,640]{2,1,0:T(8,128)(2,1)S(1)}, bf16[8,208,640]{2,1,0:T(8,128)(2,1)S(1)}, u32[]{:S(2)}, u32[]{:S(2)}) %collective-permute-start.15) | collective-permute-done | bytes 2129952 | tf_op jit(solution)/shard_map/ppermute | solution.py:36
  92.6 0.5 shard_map.87
  93.1 2.0 %collective-permute-start.16 = (bf16[2,208,640]{2,1,0:T(8,128)(2,1)S(1)}, bf16[2,208,640]{2,1,0:T(8,128)(2,1)S(1)}, u32[]{:S(2)}, u32[]{:S(2)}) collective-permute-start(bf16[2,208,640]{2,1,0:T(8,128)(2,1)S(1)} %get-tuple-element.54), channel_id=1, source_target_pairs={{0,4},{4,8},{8,12},{12,2},{2,6},{6,10},{10,14},{14,0},{1,5},{5,9},... | collective-permute-start | bytes 1597448 | tf_op jit(solution)/shard_map/ppermute | solution.py:32
  95.2 5.4 %collective-permute-start.19 = (bf16[112,640]{1,0:T(8,128)(2,1)S(1)}, bf16[112,640]{1,0:T(8,128)(2,1)S(1)}, u32[]{:S(2)}, u32[]{:S(2)}) collective-permute-start(bf16[112,640]{1,0:T(8,128)(2,1)S(1)} %get-tuple-element.59), channel_id=1, source_target_pairs={{0,10},{4,14},{8,0},{12,4},{2,8},{6,12},{10,2},{14,6},{1,11},{5,15... | collective-permute-start | bytes 430088 | tf_op jit(solution)/shard_map/ppermute | solution.py:32
  100.6 15.6 %collective-permute-done.18.up = bf16[96,640]{1,0:T(8,128)(2,1)S(1)} collective-permute-done((bf16[96,640]{1,0:T(8,128)(2,1)S(1)}, bf16[96,640]{1,0:T(8,128)(2,1)S(1)}, u32[]{:S(2)}, u32[]{:S(2)}) %collective-permute-start.18) | collective-permute-done | bytes 122912 | tf_op jit(solution)/shard_map/ppermute | solution.py:32
  116.2 0.2 shard_map.88
  116.5 0.5 collective-permute-start.23
  117.0 2.6 %collective-permute-start.20 = (bf16[208,640]{1,0:T(8,128)(2,1)S(1)}, bf16[208,640]{1,0:T(8,128)(2,1)S(1)}, u32[]{:S(2)}, u32[]{:S(2)}) collective-permute-start(bf16[208,640]{1,0:T(8,128)(2,1)S(1)} %get-tuple-element.63), channel_id=1, source_target_pairs={{0,8},{4,12},{8,2},{12,6},{2,10},{6,14},{10,0},{14,4},{1,9},{5,13}... | collective-permute-start | bytes 798728 | tf_op jit(solution)/shard_map/ppermute | solution.py:32
  119.6 1.6 collective-permute-start.21
  121.1 1.3 maximum_select_fusion.1
  122.4 1.3 maximum_select_fusion.2
  123.7 0.3 maximum_select_fusion
  124.0 0.1 fusion.2
  124.1 4.4 %collective-permute-done.20.ahead = bf16[208,640]{1,0:T(8,128)(2,1)S(1)} collective-permute-done((bf16[208,640]{1,0:T(8,128)(2,1)S(1)}, bf16[208,640]{1,0:T(8,128)(2,1)S(1)}, u32[]{:S(2)}, u32[]{:S(2)}) %collective-permute-start.20) | collective-permute-done | bytes 266272 | tf_op jit(solution)/shard_map/ppermute | solution.py:32
  128.5 0.2 collective-permute-done.21.behind
  128.7 1.0 shard_map.89
  129.7 7.6 %collective-permute-start.26 = (bf16[160,640]{1,0:T(8,128)(2,1)S(1)}, bf16[160,640]{1,0:T(8,128)(2,1)S(1)}, u32[]{:S(2)}, u32[]{:S(2)}) collective-permute-start(bf16[160,640]{1,0:T(8,128)(2,1)S(1)} %get-tuple-element.70.l0), channel_id=1, source_target_pairs={{0,14},{14,0},{4,8},{8,4},{12,2},{2,12},{10,6},{6,10},{24,20},{20,... | collective-permute-start | bytes 614408 | tf_op jit(solution)/shard_map/ppermute | solution.py:321
  137.3 0.2 copy.9.eig_g_ref
  137.5 0.7 constant_dynamic-slice_fusion.1.eig_a_ref
  138.3 1.9 %collective-permute-start.24 = (f32[20,640]{1,0:T(8,128)S(1)}, f32[20,640]{1,0:T(8,128)S(1)}, u32[]{:S(2)}, u32[]{:S(2)}) collective-permute-start(f32[20,640]{1,0:T(8,128)S(1)} %get-tuple-element.68), channel_id=1, source_target_pairs={{0,0},{14,2},{4,4},{8,6},{12,32},{2,34},{10,36},{6,38},{24,8},{20,... | collective-permute-start | bytes 153608 | tf_op jit(solution)/shard_map/ppermute | solution.py:322
  140.2 2.4 %collective-permute-done.26.l2 = bf16[160,640]{1,0:T(8,128)(2,1)S(1)} collective-permute-done((bf16[160,640]{1,0:T(8,128)(2,1)S(1)}, bf16[160,640]{1,0:T(8,128)(2,1)S(1)}, u32[]{:S(2)}, u32[]{:S(2)}) %collective-permute-start.26) | collective-permute-done | bytes 204832 | tf_op jit(solution)/shard_map/ppermute | solution.py:321
  142.7 7.2 %collective-permute-done.24 = f32[20,640]{1,0:T(8,128)S(1)} collective-permute-done((f32[20,640]{1,0:T(8,128)S(1)}, f32[20,640]{1,0:T(8,128)S(1)}, u32[]{:S(2)}, u32[]{:S(2)}) %collective-permute-start.24) | collective-permute-done | bytes 51232 | tf_op jit(solution)/shard_map/ppermute | solution.py:322
  150.0 2.2 %shard_map.90 = bf16[160,640]{1,0:T(8,128)(2,1)S(1)} custom-call(bf16[160,640]{1,0:T(8,128)(2,1)S(1)} %get-tuple-element.70.l0, bf16[160,640]{1,0:T(8,128)(2,1)S(1)} %collective-permute-done.25.l1, bf16[160,640]{1,0:T(8,128)(2,1)S(1)} %collective-permute-done.26.l2, bf16[160,640]{1,0:T(8,128)(2,1)S(1)} %collective-permute-done.27.l3, ...), custom_call_target="tpu_custom_call" | custom-call | flops 1000000000 | bytes 3000000 | tf_op jit(solution)/shard_map/pallas_call | solution.py:211
  152.2 1.9 %collective-permute-start.28 = (bf16[160,640]{1,0:T(8,128)(2,1)S(1)}, bf16[160,640]{1,0:T(8,128)(2,1)S(1)}, u32[]{:S(2)}, u32[]{:S(2)}) collective-permute-start(bf16[160,640]{1,0:T(8,128)(2,1)S(1)} %shard_map.90), channel_id=1, source_target_pairs={{0,0},{14,2},{4,4},{8,6},{12,32},{2,34},{10,36},{6,38},{24,8},{20,... | collective-permute-start | bytes 614408 | tf_op jit(solution)/shard_map/ppermute | solution.py:337
  154.1 12.1 %collective-permute-done.28 = bf16[160,640]{1,0:T(8,128)(2,1)S(1)} collective-permute-done((bf16[160,640]{1,0:T(8,128)(2,1)S(1)}, bf16[160,640]{1,0:T(8,128)(2,1)S(1)}, u32[]{:S(2)}, u32[]{:S(2)}) %collective-permute-start.28) | collective-permute-done | bytes 204832 | tf_op jit(solution)/shard_map/ppermute | solution.py:337
  166.2 0.6 copy.12
  166.8 0.7 copy.13
  (41 shorter events, 0.9 us)
Async XLA Ops:
  0.6 136.7 %copy-start = (f32[8,640]{1,0:T(8,128)S(1)}, f32[8,640]{1,0:T(8,128)}, u32[]{:S(2)}) copy-start(f32[8,640]{1,0:T(8,128)} %param.11) | copy-start | bytes 61444
  0.6 5.4 %copy-start.1 = (bf16[128,5120]{1,0:T(8,128)(2,1)S(1)}, bf16[128,5120]{1,0:T(8,128)(2,1)}, u32[]{:S(2)}) copy-start(bf16[128,5120]{1,0:T(8,128)(2,1)} %param.6) | copy-start | bytes 3932164
  3.1 16.7 %collective-permute-start.5 = (bf16[128,1280]{1,0:T(8,128)(2,1)}, bf16[128,1280]{1,0:T(8,128)(2,1)S(1)}, u32[]{:S(2)}, u32[]{:S(2)}) collective-permute-start(bf16[128,1280]{1,0:T(8,128)(2,1)} %get-tuple-element.80), channel_id=1, source_target_pairs={{0,16},{16,32},{32,48},{48,0},{1,17},{17,33},{33,49},{49,1},{2,18}... | collective-permute-start | bytes 983048 | tf_op jit(solution)/shard_map/ppermute | solution.py:49
  4.4 17.0 %collective-permute-start.6 = (bf16[128,1280]{1,0:T(8,128)(2,1)}, bf16[128,1280]{1,0:T(8,128)(2,1)}, u32[]{:S(2)}, u32[]{:S(2)}) collective-permute-start(bf16[128,1280]{1,0:T(8,128)(2,1)} %get-tuple-element.82), channel_id=1, source_target_pairs={{0,32},{16,48},{32,0},{48,16},{1,33},{17,49},{33,1},{49,17},{2,34}... | collective-permute-start | bytes 983048 | tf_op jit(solution)/shard_map/ppermute | solution.py:49
  5.0 16.7 %collective-permute-start.7 = (bf16[128,1280]{1,0:T(8,128)(2,1)}, bf16[128,1280]{1,0:T(8,128)(2,1)}, u32[]{:S(2)}, u32[]{:S(2)}) collective-permute-start(bf16[128,1280]{1,0:T(8,128)(2,1)} %get-tuple-element.81), channel_id=1, source_target_pairs={{0,48},{16,0},{32,16},{48,32},{1,49},{17,1},{33,17},{49,33},{2,50}... | collective-permute-start | bytes 983048 | tf_op jit(solution)/shard_map/ppermute | solution.py:49
  7.1 18.3 %collective-permute-start = (bf16[128,1280]{1,0:T(8,128)(2,1)}, bf16[128,1280]{1,0:T(8,128)(2,1)}, u32[]{:S(2)}, u32[]{:S(2)}) collective-permute-start(bf16[128,1280]{1,0:T(8,128)(2,1)} %get-tuple-element.84), channel_id=1, source_target_pairs={{0,64},{64,128},{128,192},{192,0},{1,65},{65,129},{129,193},{193,1... | collective-permute-start | bytes 983048 | tf_op jit(solution)/shard_map/ppermute | solution.py:49
  8.6 16.8 %collective-permute-start.1 = (bf16[128,1280]{1,0:T(8,128)(2,1)}, bf16[128,1280]{1,0:T(8,128)(2,1)}, u32[]{:S(2)}, u32[]{:S(2)}) collective-permute-start(bf16[128,1280]{1,0:T(8,128)(2,1)} %get-tuple-element.86), channel_id=1, source_target_pairs={{0,128},{64,192},{128,0},{192,64},{1,129},{65,193},{129,1},{193,65... | collective-permute-start | bytes 983048 | tf_op jit(solution)/shard_map/ppermute | solution.py:49
  19.8 0.8 copy-start.2
  19.8 8.8 %collective-permute-start.2 = (bf16[128,1280]{1,0:T(8,128)(2,1)}, bf16[128,1280]{1,0:T(8,128)(2,1)S(1)}, u32[]{:S(2)}, u32[]{:S(2)}) collective-permute-start(bf16[128,1280]{1,0:T(8,128)(2,1)} %get-tuple-element.85), channel_id=1, source_target_pairs={{0,192},{64,0},{128,64},{192,128},{1,193},{65,1},{129,65},{193,129... | collective-permute-start | bytes 983048 | tf_op jit(solution)/shard_map/ppermute | solution.py:49
  20.5 1.2 copy-start.3
  22.9 29.6 %collective-permute-start.8 = (bf16[512,1280]{1,0:T(8,128)(2,1)S(1)}, bf16[512,1280]{1,0:T(8,128)(2,1)}, u32[]{:S(2)}, u32[]{:S(2)}) collective-permute-start(bf16[512,1280]{1,0:T(8,128)(2,1)S(1)} %pad_maximum_fusion.1.refs_3_), channel_id=1, source_target_pairs={{0,64},{64,128},{128,192},{192,0},{1,65},{65,129},{129,193},{193,1... | collective-permute-start | bytes 3932168 | tf_op jit(solution)/shard_map/ppermute | solution.py:54
  24.4 30.8 %collective-permute-start.9 = (bf16[512,1280]{1,0:T(8,128)(2,1)S(1)}, bf16[512,1280]{1,0:T(8,128)(2,1)}, u32[]{:S(2)}, u32[]{:S(2)}) collective-permute-start(bf16[512,1280]{1,0:T(8,128)(2,1)S(1)} %pad_maximum_fusion.1.refs_3_), channel_id=1, source_target_pairs={{0,192},{64,0},{128,64},{192,128},{1,193},{65,1},{129,65},{193,129... | collective-permute-start | bytes 3932168 | tf_op jit(solution)/shard_map/ppermute | solution.py:54
  29.7 28.7 %collective-permute-start.3 = (bf16[512,1280]{1,0:T(8,128)(2,1)S(1)}, bf16[512,1280]{1,0:T(8,128)(2,1)}, u32[]{:S(2)}, u32[]{:S(2)}) collective-permute-start(bf16[512,1280]{1,0:T(8,128)(2,1)S(1)} %pad_maximum_fusion.refs_0_), channel_id=1, source_target_pairs={{0,16},{16,32},{32,48},{48,0},{1,17},{17,33},{33,49},{49,1},{2,18}... | collective-permute-start | bytes 3932168 | tf_op jit(solution)/shard_map/ppermute | solution.py:54
  29.8 30.9 %collective-permute-start.4 = (bf16[512,1280]{1,0:T(8,128)(2,1)S(1)}, bf16[512,1280]{1,0:T(8,128)(2,1)}, u32[]{:S(2)}, u32[]{:S(2)}) collective-permute-start(bf16[512,1280]{1,0:T(8,128)(2,1)S(1)} %pad_maximum_fusion.refs_0_), channel_id=1, source_target_pairs={{0,48},{16,0},{32,16},{48,32},{1,49},{17,1},{33,17},{49,33},{2,50}... | collective-permute-start | bytes 3932168 | tf_op jit(solution)/shard_map/ppermute | solution.py:54
  31.9 31.4 %collective-permute-start.10 = (bf16[2,160,640]{2,1,0:T(8,128)(2,1)}, bf16[2,160,640]{2,1,0:T(8,128)(2,1)S(1)}, u32[]{:S(2)}, u32[]{:S(2)}) collective-permute-start(bf16[2,160,640]{2,1,0:T(8,128)(2,1)} %get-tuple-element.39), channel_id=1, source_target_pairs={{0,2},{2,0},{1,3},{3,1},{4,6},{6,4},{5,7},{7,5},{8,10},{10,8},{9,1... | collective-permute-start | bytes 1228808 | tf_op jit(solution)/shard_map/ppermute | solution.py:36
  53.5 18.7 %collective-permute-start.13 = (bf16[256,1280]{1,0:T(8,128)(2,1)S(1)}, bf16[256,1280]{1,0:T(8,128)(2,1)S(1)}, u32[]{:S(2)}, u32[]{:S(2)}) collective-permute-start(bf16[256,1280]{1,0:T(8,128)(2,1)S(1)} %slice.29), channel_id=1, source_target_pairs={{0,64},{64,128},{128,192},{192,0},{1,65},{65,129},{129,193},{193,1... | collective-permute-start | bytes 1966088 | tf_op jit(solution)/shard_map/ppermute | solution.py:61
  56.4 15.8 %collective-permute-start.14 = (bf16[256,1280]{1,0:T(8,128)(2,1)S(1)}, bf16[256,1280]{1,0:T(8,128)(2,1)S(1)}, u32[]{:S(2)}, u32[]{:S(2)}) collective-permute-start(bf16[256,1280]{1,0:T(8,128)(2,1)S(1)} %slice.30), channel_id=1, source_target_pairs={{0,192},{64,0},{128,64},{192,128},{1,193},{65,1},{129,65},{193,129... | collective-permute-start | bytes 1966088 | tf_op jit(solution)/shard_map/ppermute | solution.py:62
  59.6 15.9 %collective-permute-start.11 = (bf16[256,1280]{1,0:T(8,128)(2,1)S(1)}, bf16[256,1280]{1,0:T(8,128)(2,1)S(1)}, u32[]{:S(2)}, u32[]{:S(2)}) collective-permute-start(bf16[256,1280]{1,0:T(8,128)(2,1)S(1)} %slice.27), channel_id=1, source_target_pairs={{0,16},{16,32},{32,48},{48,0},{1,17},{17,33},{33,49},{49,1},{2,18}... | collective-permute-start | bytes 1966088 | tf_op jit(solution)/shard_map/ppermute | solution.py:61
  61.9 17.9 %collective-permute-start.12 = (bf16[256,1280]{1,0:T(8,128)(2,1)S(1)}, bf16[256,1280]{1,0:T(8,128)(2,1)S(1)}, u32[]{:S(2)}, u32[]{:S(2)}) collective-permute-start(bf16[256,1280]{1,0:T(8,128)(2,1)S(1)} %slice.28), channel_id=1, source_target_pairs={{0,48},{16,0},{32,16},{48,32},{1,49},{17,1},{33,17},{49,33},{2,50}... | collective-permute-start | bytes 1966088 | tf_op jit(solution)/shard_map/ppermute | solution.py:62
  88.0 4.5 %collective-permute-start.15 = (bf16[8,208,640]{2,1,0:T(8,128)(2,1)S(1)}, bf16[8,208,640]{2,1,0:T(8,128)(2,1)S(1)}, u32[]{:S(2)}, u32[]{:S(2)}) collective-permute-start(bf16[8,208,640]{2,1,0:T(8,128)(2,1)S(1)} %get-tuple-element.52), channel_id=1, source_target_pairs={{0,1},{1,0},{2,3},{3,2},{4,5},{5,4},{6,7},{7,6},{8,9},{9,8},{10,11... | collective-permute-start | bytes 6389768 | tf_op jit(solution)/shard_map/ppermute | solution.py:36
  93.1 23.1 %collective-permute-start.16 = (bf16[2,208,640]{2,1,0:T(8,128)(2,1)S(1)}, bf16[2,208,640]{2,1,0:T(8,128)(2,1)S(1)}, u32[]{:S(2)}, u32[]{:S(2)}) collective-permute-start(bf16[2,208,640]{2,1,0:T(8,128)(2,1)S(1)} %get-tuple-element.54), channel_id=1, source_target_pairs={{0,4},{4,8},{8,12},{12,2},{2,6},{6,10},{10,14},{14,0},{1,5},{5,9},... | collective-permute-start | bytes 1597448 | tf_op jit(solution)/shard_map/ppermute | solution.py:32
  95.0 21.2 %collective-permute-start.17 = (bf16[2,208,640]{2,1,0:T(8,128)(2,1)S(1)}, bf16[2,208,640]{2,1,0:T(8,128)(2,1)S(1)}, u32[]{:S(2)}, u32[]{:S(2)}) collective-permute-start(bf16[2,208,640]{2,1,0:T(8,128)(2,1)S(1)} %get-tuple-element.55), channel_id=1, source_target_pairs={{0,14},{4,0},{8,4},{12,8},{2,12},{6,2},{10,6},{14,10},{1,15},{5,1}... | collective-permute-start | bytes 1597448 | tf_op jit(solution)/shard_map/ppermute | solution.py:32
  95.2 21.0 %collective-permute-start.19 = (bf16[112,640]{1,0:T(8,128)(2,1)S(1)}, bf16[112,640]{1,0:T(8,128)(2,1)S(1)}, u32[]{:S(2)}, u32[]{:S(2)}) collective-permute-start(bf16[112,640]{1,0:T(8,128)(2,1)S(1)} %get-tuple-element.59), channel_id=1, source_target_pairs={{0,10},{4,14},{8,0},{12,4},{2,8},{6,12},{10,2},{14,6},{1,11},{5,15... | collective-permute-start | bytes 430088 | tf_op jit(solution)/shard_map/ppermute | solution.py:32
  100.6 15.6 %collective-permute-start.18 = (bf16[96,640]{1,0:T(8,128)(2,1)S(1)}, bf16[96,640]{1,0:T(8,128)(2,1)S(1)}, u32[]{:S(2)}, u32[]{:S(2)}) collective-permute-start(bf16[96,640]{1,0:T(8,128)(2,1)S(1)} %get-tuple-element.58), channel_id=1, source_target_pairs={{0,8},{4,12},{8,2},{12,6},{2,10},{6,14},{10,0},{14,4},{1,9},{5,13}... | collective-permute-start | bytes 368648 | tf_op jit(solution)/shard_map/ppermute | solution.py:32
  116.4 4.7 %collective-permute-start.22 = (bf16[2,160,640]{2,1,0:T(8,128)(2,1)S(1)}, bf16[2,160,640]{2,1,0:T(8,128)(2,1)}, u32[]{:S(2)}, u32[]{:S(2)}) collective-permute-start(bf16[2,160,640]{2,1,0:T(8,128)(2,1)S(1)} %get-tuple-element.65), channel_id=1, source_target_pairs={{0,1},{1,0},{2,3},{3,2},{4,5},{5,4},{6,7},{7,6},{8,9},{9,8},{10,11... | collective-permute-start | bytes 1228808 | tf_op jit(solution)/shard_map/ppermute | solution.py:36
  116.5 5.9 %collective-permute-start.23 = (bf16[2,160,640]{2,1,0:T(8,128)(2,1)S(1)}, bf16[2,160,640]{2,1,0:T(8,128)(2,1)}, u32[]{:S(2)}, u32[]{:S(2)}) collective-permute-start(bf16[2,160,640]{2,1,0:T(8,128)(2,1)S(1)} %collective-permute-done.10), channel_id=1, source_target_pairs={{0,1},{1,0},{2,3},{3,2},{4,5},{5,4},{6,7},{7,6},{8,9},{9,8},{10,11... | collective-permute-start | bytes 1228808 | tf_op jit(solution)/shard_map/ppermute | solution.py:36
  117.0 11.5 %collective-permute-start.20 = (bf16[208,640]{1,0:T(8,128)(2,1)S(1)}, bf16[208,640]{1,0:T(8,128)(2,1)S(1)}, u32[]{:S(2)}, u32[]{:S(2)}) collective-permute-start(bf16[208,640]{1,0:T(8,128)(2,1)S(1)} %get-tuple-element.63), channel_id=1, source_target_pairs={{0,8},{4,12},{8,2},{12,6},{2,10},{6,14},{10,0},{14,4},{1,9},{5,13}... | collective-permute-start | bytes 798728 | tf_op jit(solution)/shard_map/ppermute | solution.py:32
  119.6 9.2 %collective-permute-start.21 = (bf16[208,640]{1,0:T(8,128)(2,1)S(1)}, bf16[208,640]{1,0:T(8,128)(2,1)S(1)}, u32[]{:S(2)}, u32[]{:S(2)}) collective-permute-start(bf16[208,640]{1,0:T(8,128)(2,1)S(1)} %get-tuple-element.64), channel_id=1, source_target_pairs={{0,10},{4,14},{8,0},{12,4},{2,8},{6,12},{10,2},{14,6},{1,11},{5,15... | collective-permute-start | bytes 798728 | tf_op jit(solution)/shard_map/ppermute | solution.py:32
  129.7 12.9 %collective-permute-start.26 = (bf16[160,640]{1,0:T(8,128)(2,1)S(1)}, bf16[160,640]{1,0:T(8,128)(2,1)S(1)}, u32[]{:S(2)}, u32[]{:S(2)}) collective-permute-start(bf16[160,640]{1,0:T(8,128)(2,1)S(1)} %get-tuple-element.70.l0), channel_id=1, source_target_pairs={{0,14},{14,0},{4,8},{8,4},{12,2},{2,12},{10,6},{6,10},{24,20},{20,... | collective-permute-start | bytes 614408 | tf_op jit(solution)/shard_map/ppermute | solution.py:321
  138.3 11.7 %collective-permute-start.25 = (bf16[160,640]{1,0:T(8,128)(2,1)S(1)}, bf16[160,640]{1,0:T(8,128)(2,1)S(1)}, u32[]{:S(2)}, u32[]{:S(2)}) collective-permute-start(bf16[160,640]{1,0:T(8,128)(2,1)S(1)} %get-tuple-element.70.l0), channel_id=1, source_target_pairs={{0,1},{1,0},{2,3},{3,2},{4,5},{5,4},{6,7},{7,6},{8,9},{9,8},{10,11... | collective-permute-start | bytes 614408 | tf_op jit(solution)/shard_map/ppermute | solution.py:36
  138.3 11.7 %collective-permute-start.24 = (f32[20,640]{1,0:T(8,128)S(1)}, f32[20,640]{1,0:T(8,128)S(1)}, u32[]{:S(2)}, u32[]{:S(2)}) collective-permute-start(f32[20,640]{1,0:T(8,128)S(1)} %get-tuple-element.68), channel_id=1, source_target_pairs={{0,0},{14,2},{4,4},{8,6},{12,32},{2,34},{10,36},{6,38},{24,8},{20,... | collective-permute-start | bytes 153608 | tf_op jit(solution)/shard_map/ppermute | solution.py:322
  142.5 7.4 %collective-permute-start.27 = (bf16[160,640]{1,0:T(8,128)(2,1)S(1)}, bf16[160,640]{1,0:T(8,128)(2,1)S(1)}, u32[]{:S(2)}, u32[]{:S(2)}) collective-permute-start(bf16[160,640]{1,0:T(8,128)(2,1)S(1)} %collective-permute-done.26.l2), channel_id=1, source_target_pairs={{0,1},{1,0},{2,3},{3,2},{4,5},{5,4},{6,7},{7,6},{8,9},{9,8},{10,11... | collective-permute-start | bytes 614408 | tf_op jit(solution)/shard_map/ppermute | solution.py:36
  152.2 14.0 %collective-permute-start.28 = (bf16[160,640]{1,0:T(8,128)(2,1)S(1)}, bf16[160,640]{1,0:T(8,128)(2,1)S(1)}, u32[]{:S(2)}, u32[]{:S(2)}) collective-permute-start(bf16[160,640]{1,0:T(8,128)(2,1)S(1)} %shard_map.90), channel_id=1, source_target_pairs={{0,0},{14,2},{4,4},{8,6},{12,32},{2,34},{10,36},{6,38},{24,8},{20,... | collective-permute-start | bytes 614408 | tf_op jit(solution)/shard_map/ppermute | solution.py:337

commit v2 on v1

--- a/solution.py
+++ b/solution.py
@@ -320,7 +320,6 @@
             moves.append((at, ((2 * b + y0 // 2) * 4 + 2 * (y0 % 2) + c) * 2 + h))
     left_far = lax.ppermute(left, ("y", "zl", "zh"), pairs)
     factor_g = lax.ppermute(factor_g, ("y", "zl", "zh"), moves)
-    qg, qa, factor_g = lax.optimization_barrier((qg, qa, factor_g))
     result = call(
         finish_kernel,
         [((160, 640), BF16)],
@@ -334,6 +333,7 @@
         10**9,
         3 * 10**6,
     )
+    result, factor_g = lax.optimization_barrier((result, factor_g))
     result = lax.ppermute(result, ("y", "zl", "zh"), moves)
     return factor_a, factor_g, result.T[None]
 

time: 168 us -> 166 us (0.988)
  waiting for transfers between devices: 80.4 us -> 78.2 us
    ppermute x1, waiting for transfers between devices: 7.22 us -> 3.75 us  [body(): factor_g = lax.ppermute(factor_g, ('y', 'zl', 'zh'), moves)]
  transfers between devices with their start and end apart: 29 -> 29, of which waited for: 15 -> 16; matrix products, arithmetic and copies ran while one was open for 9% -> 9% of each run, Pallas kernels for 5% -> 7%
where the time goes in v2:
time: 166 us; the launch traced here: 165 us
  waiting for transfers between devices  78.2 us (47%)
  starting transfers between devices  45.8 us (28%)
  Pallas kernels  20.9 us (13%)
  local copies, waits for them, and re-layouts  12.9 us (8%)
  other arithmetic  6.52 us (4%)
    pallas_call x6, Pallas kernels, call(): pl.pallas_call(kernel, out_shape=shapes, in_specs=([] if scalars is None...  20.9 us
    ppermute x6, waiting for transfers between devices, to_z(): return lax.ppermute(array, ('zl', 'zh'), z_shift(by))  20.2 us
    ppermute x2, waiting for transfers between devices, gather_near(): lax.ppermute(own, axis, shift(4, 1))  15.2 us
    ppermute x1, waiting for transfers between devices, body(): result = lax.ppermute(result, ('y', 'zl', 'zh'), moves)  12.1 us
    ppermute x6, starting transfers between devices, to_z(): return lax.ppermute(array, ('zl', 'zh'), z_shift(by))  11.6 us
    ppermute x6, waiting for transfers between devices, exchange(): got[d] = cols if d == 0 else lax.ppermute(cols, axis, shift(count, d))  11.5 us
    ppermute x1, starting transfers between devices, body(): left_far = lax.ppermute(left, ('y', 'zl', 'zh'), pairs)  7.63 us
    ppermute x6, starting transfers between devices, swap(): return lax.ppermute(array, axis, shift(2, 1))  7.28 us
  transfers between devices with their start and end apart: 29, of which 16 were waited for; matrix products, arithmetic and copies ran while one was open for 9% of the time, Pallas kernels for 7%

profile of v2, /device:TPU:50, one launch (start us, length us, event | category | flops | bytes accessed | tf_op | source)
XLA Modules:
  0.0 165.3 jit_solution(2883493514805427951)
XLA Ops:
  0.7 2.4 %constant_dynamic-slice_fusion.5 = (bf16[128,1280]{1,0:T(8,128)(2,1)S(1)}, bf16[128,1280]{1,0:T(8,128)(2,1)}, bf16[128,1280]{1,0:T(8,128)(2,1)}, bf16[128,1280]{1,0:T(8,128)(2,1)}) fusion(bf16[128,5120]{1,0:T(8,128)(2,1)} %param.7, s32[]{:T(128)S(6)} %select_n.778, s32[]{:T(128)S(6)} %select_n.779, s32[]{:T(128)S(6)} %select_n.781, s32[]{:T(128)S(6)} %select_n.780), kind=kLoop, calls=%fused_computation.20 | loop fusion | bytes 2621456 | tf_op jit(solution)/shard_map/dynamic_slice | solution.py:48
  3.1 1.3 collective-permute-start.5
  4.4 0.6 collective-permute-start.6
  5.0 1.1 collective-permute-start.7
  6.0 1.0 constant_dynamic-slice_fusion.9
  7.1 1.5 collective-permute-start
  8.6 1.1 collective-permute-start.1
  9.7 1.1 constant_dynamic-slice_fusion.11
  10.8 1.1 constant_dynamic-slice_fusion.10
  11.8 7.9 %collective-permute-done.5 = bf16[128,1280]{1,0:T(8,128)(2,1)S(1)} collective-permute-done((bf16[128,1280]{1,0:T(8,128)(2,1)}, bf16[128,1280]{1,0:T(8,128)(2,1)S(1)}, u32[]{:S(2)}, u32[]{:S(2)}) %collective-permute-start.5) | collective-permute-done | bytes 327712 | tf_op jit(solution)/shard_map/ppermute | solution.py:49
  19.8 0.5 collective-permute-start.2
  20.3 0.2 copy-done.2
  20.5 0.9 pad_maximum_fusion.3
  21.4 0.3 collective-permute-done.7
  21.7 1.2 pad_maximum_fusion.1.refs_3_
  22.9 1.6 collective-permute-start.8
  24.4 0.9 collective-permute-start.9
  25.4 3.2 %collective-permute-done.2 = bf16[128,1280]{1,0:T(8,128)(2,1)S(1)} collective-permute-done((bf16[128,1280]{1,0:T(8,128)(2,1)}, bf16[128,1280]{1,0:T(8,128)(2,1)S(1)}, u32[]{:S(2)}, u32[]{:S(2)}) %collective-permute-start.2) | collective-permute-done | bytes 327712 | tf_op jit(solution)/shard_map/ppermute | solution.py:49
  28.6 1.2 pad_maximum_fusion.refs_0_
  29.8 2.0 %collective-permute-start.4 = (bf16[512,1280]{1,0:T(8,128)(2,1)S(1)}, bf16[512,1280]{1,0:T(8,128)(2,1)}, u32[]{:S(2)}, u32[]{:S(2)}) collective-permute-start(bf16[512,1280]{1,0:T(8,128)(2,1)S(1)} %pad_maximum_fusion.refs_0_), channel_id=1, source_target_pairs={{0,48},{16,0},{32,16},{48,32},{1,49},{17,1},{33,17},{49,33},{2,50}... | collective-permute-start | bytes 3932168 | tf_op jit(solution)/shard_map/ppermute | solution.py:54
  31.9 6.4 %collective-permute-start.10 = (bf16[2,160,640]{2,1,0:T(8,128)(2,1)}, bf16[2,160,640]{2,1,0:T(8,128)(2,1)S(1)}, u32[]{:S(2)}, u32[]{:S(2)}) collective-permute-start(bf16[2,160,640]{2,1,0:T(8,128)(2,1)} %get-tuple-element.38), channel_id=1, source_target_pairs={{0,2},{2,0},{1,3},{3,1},{4,6},{6,4},{5,7},{7,5},{8,10},{10,8},{9,1... | collective-permute-start | bytes 1228808 | tf_op jit(solution)/shard_map/ppermute | solution.py:36
  38.5 13.9 %collective-permute-done.8.refs_4_ = bf16[512,1280]{1,0:T(8,128)(2,1)} collective-permute-done((bf16[512,1280]{1,0:T(8,128)(2,1)S(1)}, bf16[512,1280]{1,0:T(8,128)(2,1)}, u32[]{:S(2)}, u32[]{:S(2)}) %collective-permute-start.8) | collective-permute-done | bytes 1310752 | tf_op jit(solution)/shard_map/ppermute | solution.py:54
  52.4 1.1 slice.29
  53.5 1.6 collective-permute-start.13
  55.2 1.1 slice.30
  56.4 0.8 collective-permute-start.14
  57.1 1.3 collective-permute-done.3.refs_1_
  58.5 1.1 slice.27
  59.6 1.2 collective-permute-start.11
  60.8 1.1 slice.28
  61.9 1.2 collective-permute-start.12
  63.1 0.3 fusion.order_ref
  63.4 8.8 %shard_map.85 = (f32[2,640,1280]{2,1,0:T(8,128)S(1)}, f32[896,640]{1,0:T(8,128)S(1)}, bf16[384,1280]{1,0:T(8,128)(2,1)S(1)}, bf16[384,1280]{1,0:T(8,128)(2,1)S(1)}) custom-call(s32[5]{0:T(128)S(1)} %stack.74.where_ref, bf16[512,1280]{1,0:T(8,128)(2,1)S(1)} %pad_maximum_fusion.refs_0_, bf16[512,1280]{1,0:T(8,128)(2,1)} %collective-permute-done.3.refs_1_, ...), custom_call_target="tpu_custom_call" | custom-call | flops 5000000000 | bytes 10000000 | tf_op jit(solution)/shard_map/pallas_call | solution.py:211
  72.2 3.3 %collective-permute-done.11.al = bf16[256,1280]{1,0:T(8,128)(2,1)S(1)} collective-permute-done((bf16[256,1280]{1,0:T(8,128)(2,1)S(1)}, bf16[256,1280]{1,0:T(8,128)(2,1)S(1)}, u32[]{:S(2)}, u32[]{:S(2)}) %collective-permute-start.11) | collective-permute-done | bytes 655392 | tf_op jit(solution)/shard_map/ppermute | solution.py:61
  75.5 4.3 %collective-permute-done.12.ah = bf16[256,1280]{1,0:T(8,128)(2,1)S(1)} collective-permute-done((bf16[256,1280]{1,0:T(8,128)(2,1)S(1)}, bf16[256,1280]{1,0:T(8,128)(2,1)S(1)}, u32[]{:S(2)}, u32[]{:S(2)}) %collective-permute-start.12) | collective-permute-done | bytes 655392 | tf_op jit(solution)/shard_map/ppermute | solution.py:62
  79.8 8.3 %shard_map.86 = (bf16[8,208,640]{2,1,0:T(8,128)(2,1)S(1)}, bf16[8,208,640]{2,1,0:T(8,128)(2,1)S(1)}) custom-call(s32[5]{0:T(128)S(1)} %stack.74.where_ref, bf16[384,1280]{1,0:T(8,128)(2,1)S(1)} %get-tuple-element.45.acts_mid, bf16[384,1280]{1,0:T(8,128)(2,1)S(1)} %get-tuple-element.46.grads_mid, bf16[256,1280]{1,0:T(8,128)(2,1)S(1)} %collective-permute-done.11.al, ...), custom_call_target="tpu_custom_call" | custom-call | flops 4000000000 | bytes 10000000 | tf_op jit(solution)/shard_map/pallas_call | solution.py:211
  88.0 0.3 collective-permute-start.15
  88.4 4.2 %collective-permute-done.15.came = bf16[8,208,640]{2,1,0:T(8,128)(2,1)S(1)} collective-permute-done((bf16[8,208,640]{2,1,0:T(8,128)(2,1)S(1)}, bf16[8,208,640]{2,1,0:T(8,128)(2,1)S(1)}, u32[]{:S(2)}, u32[]{:S(2)}) %collective-permute-start.15) | collective-permute-done | bytes 2129952 | tf_op jit(solution)/shard_map/ppermute | solution.py:36
  92.6 0.5 shard_map.87
  93.1 2.0 %collective-permute-start.16 = (bf16[2,208,640]{2,1,0:T(8,128)(2,1)S(1)}, bf16[2,208,640]{2,1,0:T(8,128)(2,1)S(1)}, u32[]{:S(2)}, u32[]{:S(2)}) collective-permute-start(bf16[2,208,640]{2,1,0:T(8,128)(2,1)S(1)} %get-tuple-element.53), channel_id=1, source_target_pairs={{0,4},{4,8},{8,12},{12,2},{2,6},{6,10},{10,14},{14,0},{1,5},{5,9},... | collective-permute-start | bytes 1597448 | tf_op jit(solution)/shard_map/ppermute | solution.py:32
  95.2 5.4 %collective-permute-start.19 = (bf16[112,640]{1,0:T(8,128)(2,1)S(1)}, bf16[112,640]{1,0:T(8,128)(2,1)S(1)}, u32[]{:S(2)}, u32[]{:S(2)}) collective-permute-start(bf16[112,640]{1,0:T(8,128)(2,1)S(1)} %get-tuple-element.58), channel_id=1, source_target_pairs={{0,10},{4,14},{8,0},{12,4},{2,8},{6,12},{10,2},{14,6},{1,11},{5,15... | collective-permute-start | bytes 430088 | tf_op jit(solution)/shard_map/ppermute | solution.py:32
  100.6 15.6 %collective-permute-done.18.up = bf16[96,640]{1,0:T(8,128)(2,1)S(1)} collective-permute-done((bf16[96,640]{1,0:T(8,128)(2,1)S(1)}, bf16[96,640]{1,0:T(8,128)(2,1)S(1)}, u32[]{:S(2)}, u32[]{:S(2)}) %collective-permute-start.18) | collective-permute-done | bytes 122912 | tf_op jit(solution)/shard_map/ppermute | solution.py:32
  116.2 0.2 shard_map.88
  116.5 0.5 collective-permute-start.23
  117.0 2.6 %collective-permute-start.20 = (bf16[208,640]{1,0:T(8,128)(2,1)S(1)}, bf16[208,640]{1,0:T(8,128)(2,1)S(1)}, u32[]{:S(2)}, u32[]{:S(2)}) collective-permute-start(bf16[208,640]{1,0:T(8,128)(2,1)S(1)} %get-tuple-element.62), channel_id=1, source_target_pairs={{0,8},{4,12},{8,2},{12,6},{2,10},{6,14},{10,0},{14,4},{1,9},{5,13}... | collective-permute-start | bytes 798728 | tf_op jit(solution)/shard_map/ppermute | solution.py:32
  119.6 1.6 collective-permute-start.21
  121.1 1.3 maximum_select_fusion.1
  122.4 1.3 maximum_select_fusion.2
  123.7 0.3 maximum_select_fusion
  124.1 4.4 %collective-permute-done.20.ahead = bf16[208,640]{1,0:T(8,128)(2,1)S(1)} collective-permute-done((bf16[208,640]{1,0:T(8,128)(2,1)S(1)}, bf16[208,640]{1,0:T(8,128)(2,1)S(1)}, u32[]{:S(2)}, u32[]{:S(2)}) %collective-permute-start.20) | collective-permute-done | bytes 266272 | tf_op jit(solution)/shard_map/ppermute | solution.py:32
  128.5 0.2 collective-permute-done.21.behind
  128.7 1.0 shard_map.89
  129.7 7.6 %collective-permute-start.25 = (bf16[160,640]{1,0:T(8,128)(2,1)S(1)}, bf16[160,640]{1,0:T(8,128)(2,1)S(1)}, u32[]{:S(2)}, u32[]{:S(2)}) collective-permute-start(bf16[160,640]{1,0:T(8,128)(2,1)S(1)} %get-tuple-element.67.l0), channel_id=1, source_target_pairs={{0,14},{14,0},{4,8},{8,4},{12,2},{2,12},{10,6},{6,10},{24,20},{20,... | collective-permute-start | bytes 614408 | tf_op jit(solution)/shard_map/ppermute | solution.py:321
  137.3 0.2 copy.9.eig_g_ref
  137.5 0.7 constant_dynamic-slice_fusion.1.eig_a_ref
  138.3 1.9 %collective-permute-start.27 = (f32[20,640]{1,0:T(8,128)S(1)}, f32[20,640]{1,0:T(8,128)S(1)}, u32[]{:S(2)}, u32[]{:S(2)}) collective-permute-start(f32[20,640]{1,0:T(8,128)S(1)} %get-tuple-element.68), channel_id=1, source_target_pairs={{0,0},{14,2},{4,4},{8,6},{12,32},{2,34},{10,36},{6,38},{24,8},{20,... | collective-permute-start | bytes 153608 | tf_op jit(solution)/shard_map/ppermute | solution.py:322
  140.2 2.4 %collective-permute-done.25.l2 = bf16[160,640]{1,0:T(8,128)(2,1)S(1)} collective-permute-done((bf16[160,640]{1,0:T(8,128)(2,1)S(1)}, bf16[160,640]{1,0:T(8,128)(2,1)S(1)}, u32[]{:S(2)}, u32[]{:S(2)}) %collective-permute-start.25) | collective-permute-done | bytes 204832 | tf_op jit(solution)/shard_map/ppermute | solution.py:321
  142.8 1.2 collective-permute-done.26.l3
  144.0 2.2 %shard_map.90 = bf16[160,640]{1,0:T(8,128)(2,1)S(1)} custom-call(bf16[160,640]{1,0:T(8,128)(2,1)S(1)} %get-tuple-element.67.l0, bf16[160,640]{1,0:T(8,128)(2,1)S(1)} %collective-permute-done.24.l1, bf16[160,640]{1,0:T(8,128)(2,1)S(1)} %collective-permute-done.25.l2, bf16[160,640]{1,0:T(8,128)(2,1)S(1)} %collective-permute-done.26.l3, ...), custom_call_target="tpu_custom_call" | custom-call | flops 1000000000 | bytes 3000000 | tf_op jit(solution)/shard_map/pallas_call | solution.py:211
  146.2 3.7 %collective-permute-done.27 = f32[20,640]{1,0:T(8,128)S(1)} collective-permute-done((f32[20,640]{1,0:T(8,128)S(1)}, f32[20,640]{1,0:T(8,128)S(1)}, u32[]{:S(2)}, u32[]{:S(2)}) %collective-permute-start.27) | collective-permute-done | bytes 51232 | tf_op jit(solution)/shard_map/ppermute | solution.py:322
  150.0 1.9 %collective-permute-start.28 = (bf16[160,640]{1,0:T(8,128)(2,1)S(1)}, bf16[160,640]{1,0:T(8,128)(2,1)S(1)}, u32[]{:S(2)}, u32[]{:S(2)}) collective-permute-start(bf16[160,640]{1,0:T(8,128)(2,1)S(1)} %shard_map.90), channel_id=1, source_target_pairs={{0,0},{14,2},{4,4},{8,6},{12,32},{2,34},{10,36},{6,38},{24,8},{20,... | collective-permute-start | bytes 614408 | tf_op jit(solution)/shard_map/ppermute | solution.py:337
  151.9 12.1 %collective-permute-done.28 = bf16[160,640]{1,0:T(8,128)(2,1)S(1)} collective-permute-done((bf16[160,640]{1,0:T(8,128)(2,1)S(1)}, bf16[160,640]{1,0:T(8,128)(2,1)S(1)}, u32[]{:S(2)}, u32[]{:S(2)}) %collective-permute-start.28) | collective-permute-done | bytes 204832 | tf_op jit(solution)/shard_map/ppermute | solution.py:337
  164.0 0.6 copy.12
  164.6 0.7 copy.13
  (41 shorter events, 1.1 us)
Async XLA Ops:
  0.6 136.7 %copy-start = (f32[8,640]{1,0:T(8,128)S(1)}, f32[8,640]{1,0:T(8,128)}, u32[]{:S(2)}) copy-start(f32[8,640]{1,0:T(8,128)} %param.11) | copy-start | bytes 61444
  0.6 5.4 %copy-start.1 = (bf16[128,5120]{1,0:T(8,128)(2,1)S(1)}, bf16[128,5120]{1,0:T(8,128)(2,1)}, u32[]{:S(2)}) copy-start(bf16[128,5120]{1,0:T(8,128)(2,1)} %param.6) | copy-start | bytes 3932164
  3.1 16.7 %collective-permute-start.5 = (bf16[128,1280]{1,0:T(8,128)(2,1)}, bf16[128,1280]{1,0:T(8,128)(2,1)S(1)}, u32[]{:S(2)}, u32[]{:S(2)}) collective-permute-start(bf16[128,1280]{1,0:T(8,128)(2,1)} %get-tuple-element.78), channel_id=1, source_target_pairs={{0,16},{16,32},{32,48},{48,0},{1,17},{17,33},{33,49},{49,1},{2,18}... | collective-permute-start | bytes 983048 | tf_op jit(solution)/shard_map/ppermute | solution.py:49
  4.4 17.0 %collective-permute-start.6 = (bf16[128,1280]{1,0:T(8,128)(2,1)}, bf16[128,1280]{1,0:T(8,128)(2,1)}, u32[]{:S(2)}, u32[]{:S(2)}) collective-permute-start(bf16[128,1280]{1,0:T(8,128)(2,1)} %get-tuple-element.80), channel_id=1, source_target_pairs={{0,32},{16,48},{32,0},{48,16},{1,33},{17,49},{33,1},{49,17},{2,34}... | collective-permute-start | bytes 983048 | tf_op jit(solution)/shard_map/ppermute | solution.py:49
  5.0 16.7 %collective-permute-start.7 = (bf16[128,1280]{1,0:T(8,128)(2,1)}, bf16[128,1280]{1,0:T(8,128)(2,1)}, u32[]{:S(2)}, u32[]{:S(2)}) collective-permute-start(bf16[128,1280]{1,0:T(8,128)(2,1)} %get-tuple-element.79), channel_id=1, source_target_pairs={{0,48},{16,0},{32,16},{48,32},{1,49},{17,1},{33,17},{49,33},{2,50}... | collective-permute-start | bytes 983048 | tf_op jit(solution)/shard_map/ppermute | solution.py:49
  7.1 18.3 %collective-permute-start = (bf16[128,1280]{1,0:T(8,128)(2,1)}, bf16[128,1280]{1,0:T(8,128)(2,1)}, u32[]{:S(2)}, u32[]{:S(2)}) collective-permute-start(bf16[128,1280]{1,0:T(8,128)(2,1)} %get-tuple-element.82), channel_id=1, source_target_pairs={{0,64},{64,128},{128,192},{192,0},{1,65},{65,129},{129,193},{193,1... | collective-permute-start | bytes 983048 | tf_op jit(solution)/shard_map/ppermute | solution.py:49
  8.6 16.8 %collective-permute-start.1 = (bf16[128,1280]{1,0:T(8,128)(2,1)}, bf16[128,1280]{1,0:T(8,128)(2,1)}, u32[]{:S(2)}, u32[]{:S(2)}) collective-permute-start(bf16[128,1280]{1,0:T(8,128)(2,1)} %get-tuple-element.84), channel_id=1, source_target_pairs={{0,128},{64,192},{128,0},{192,64},{1,129},{65,193},{129,1},{193,65... | collective-permute-start | bytes 983048 | tf_op jit(solution)/shard_map/ppermute | solution.py:49
  19.8 0.8 copy-start.2
  19.8 8.8 %collective-permute-start.2 = (bf16[128,1280]{1,0:T(8,128)(2,1)}, bf16[128,1280]{1,0:T(8,128)(2,1)S(1)}, u32[]{:S(2)}, u32[]{:S(2)}) collective-permute-start(bf16[128,1280]{1,0:T(8,128)(2,1)} %get-tuple-element.83), channel_id=1, source_target_pairs={{0,192},{64,0},{128,64},{192,128},{1,193},{65,1},{129,65},{193,129... | collective-permute-start | bytes 983048 | tf_op jit(solution)/shard_map/ppermute | solution.py:49
  20.5 1.2 copy-start.3
  22.9 29.6 %collective-permute-start.8 = (bf16[512,1280]{1,0:T(8,128)(2,1)S(1)}, bf16[512,1280]{1,0:T(8,128)(2,1)}, u32[]{:S(2)}, u32[]{:S(2)}) collective-permute-start(bf16[512,1280]{1,0:T(8,128)(2,1)S(1)} %pad_maximum_fusion.1.refs_3_), channel_id=1, source_target_pairs={{0,64},{64,128},{128,192},{192,0},{1,65},{65,129},{129,193},{193,1... | collective-permute-start | bytes 3932168 | tf_op jit(solution)/shard_map/ppermute | solution.py:54
  24.4 30.8 %collective-permute-start.9 = (bf16[512,1280]{1,0:T(8,128)(2,1)S(1)}, bf16[512,1280]{1,0:T(8,128)(2,1)}, u32[]{:S(2)}, u32[]{:S(2)}) collective-permute-start(bf16[512,1280]{1,0:T(8,128)(2,1)S(1)} %pad_maximum_fusion.1.refs_3_), channel_id=1, source_target_pairs={{0,192},{64,0},{128,64},{192,128},{1,193},{65,1},{129,65},{193,129... | collective-permute-start | bytes 3932168 | tf_op jit(solution)/shard_map/ppermute | solution.py:54
  29.7 28.7 %collective-permute-start.3 = (bf16[512,1280]{1,0:T(8,128)(2,1)S(1)}, bf16[512,1280]{1,0:T(8,128)(2,1)}, u32[]{:S(2)}, u32[]{:S(2)}) collective-permute-start(bf16[512,1280]{1,0:T(8,128)(2,1)S(1)} %pad_maximum_fusion.refs_0_), channel_id=1, source_target_pairs={{0,16},{16,32},{32,48},{48,0},{1,17},{17,33},{33,49},{49,1},{2,18}... | collective-permute-start | bytes 3932168 | tf_op jit(solution)/shard_map/ppermute | solution.py:54
  29.8 30.9 %collective-permute-start.4 = (bf16[512,1280]{1,0:T(8,128)(2,1)S(1)}, bf16[512,1280]{1,0:T(8,128)(2,1)}, u32[]{:S(2)}, u32[]{:S(2)}) collective-permute-start(bf16[512,1280]{1,0:T(8,128)(2,1)S(1)} %pad_maximum_fusion.refs_0_), channel_id=1, source_target_pairs={{0,48},{16,0},{32,16},{48,32},{1,49},{17,1},{33,17},{49,33},{2,50}... | collective-permute-start | bytes 3932168 | tf_op jit(solution)/shard_map/ppermute | solution.py:54
  31.9 31.4 %collective-permute-start.10 = (bf16[2,160,640]{2,1,0:T(8,128)(2,1)}, bf16[2,160,640]{2,1,0:T(8,128)(2,1)S(1)}, u32[]{:S(2)}, u32[]{:S(2)}) collective-permute-start(bf16[2,160,640]{2,1,0:T(8,128)(2,1)} %get-tuple-element.38), channel_id=1, source_target_pairs={{0,2},{2,0},{1,3},{3,1},{4,6},{6,4},{5,7},{7,5},{8,10},{10,8},{9,1... | collective-permute-start | bytes 1228808 | tf_op jit(solution)/shard_map/ppermute | solution.py:36
  53.5 18.7 %collective-permute-start.13 = (bf16[256,1280]{1,0:T(8,128)(2,1)S(1)}, bf16[256,1280]{1,0:T(8,128)(2,1)S(1)}, u32[]{:S(2)}, u32[]{:S(2)}) collective-permute-start(bf16[256,1280]{1,0:T(8,128)(2,1)S(1)} %slice.29), channel_id=1, source_target_pairs={{0,64},{64,128},{128,192},{192,0},{1,65},{65,129},{129,193},{193,1... | collective-permute-start | bytes 1966088 | tf_op jit(solution)/shard_map/ppermute | solution.py:61
  56.4 15.8 %collective-permute-start.14 = (bf16[256,1280]{1,0:T(8,128)(2,1)S(1)}, bf16[256,1280]{1,0:T(8,128)(2,1)S(1)}, u32[]{:S(2)}, u32[]{:S(2)}) collective-permute-start(bf16[256,1280]{1,0:T(8,128)(2,1)S(1)} %slice.30), channel_id=1, source_target_pairs={{0,192},{64,0},{128,64},{192,128},{1,193},{65,1},{129,65},{193,129... | collective-permute-start | bytes 1966088 | tf_op jit(solution)/shard_map/ppermute | solution.py:62
  59.6 15.9 %collective-permute-start.11 = (bf16[256,1280]{1,0:T(8,128)(2,1)S(1)}, bf16[256,1280]{1,0:T(8,128)(2,1)S(1)}, u32[]{:S(2)}, u32[]{:S(2)}) collective-permute-start(bf16[256,1280]{1,0:T(8,128)(2,1)S(1)} %slice.27), channel_id=1, source_target_pairs={{0,16},{16,32},{32,48},{48,0},{1,17},{17,33},{33,49},{49,1},{2,18}... | collective-permute-start | bytes 1966088 | tf_op jit(solution)/shard_map/ppermute | solution.py:61
  61.9 17.9 %collective-permute-start.12 = (bf16[256,1280]{1,0:T(8,128)(2,1)S(1)}, bf16[256,1280]{1,0:T(8,128)(2,1)S(1)}, u32[]{:S(2)}, u32[]{:S(2)}) collective-permute-start(bf16[256,1280]{1,0:T(8,128)(2,1)S(1)} %slice.28), channel_id=1, source_target_pairs={{0,48},{16,0},{32,16},{48,32},{1,49},{17,1},{33,17},{49,33},{2,50}... | collective-permute-start | bytes 1966088 | tf_op jit(solution)/shard_map/ppermute | solution.py:62
  88.0 4.5 %collective-permute-start.15 = (bf16[8,208,640]{2,1,0:T(8,128)(2,1)S(1)}, bf16[8,208,640]{2,1,0:T(8,128)(2,1)S(1)}, u32[]{:S(2)}, u32[]{:S(2)}) collective-permute-start(bf16[8,208,640]{2,1,0:T(8,128)(2,1)S(1)} %get-tuple-element.51), channel_id=1, source_target_pairs={{0,1},{1,0},{2,3},{3,2},{4,5},{5,4},{6,7},{7,6},{8,9},{9,8},{10,11... | collective-permute-start | bytes 6389768 | tf_op jit(solution)/shard_map/ppermute | solution.py:36
  93.1 23.1 %collective-permute-start.16 = (bf16[2,208,640]{2,1,0:T(8,128)(2,1)S(1)}, bf16[2,208,640]{2,1,0:T(8,128)(2,1)S(1)}, u32[]{:S(2)}, u32[]{:S(2)}) collective-permute-start(bf16[2,208,640]{2,1,0:T(8,128)(2,1)S(1)} %get-tuple-element.53), channel_id=1, source_target_pairs={{0,4},{4,8},{8,12},{12,2},{2,6},{6,10},{10,14},{14,0},{1,5},{5,9},... | collective-permute-start | bytes 1597448 | tf_op jit(solution)/shard_map/ppermute | solution.py:32
  95.0 21.2 %collective-permute-start.17 = (bf16[2,208,640]{2,1,0:T(8,128)(2,1)S(1)}, bf16[2,208,640]{2,1,0:T(8,128)(2,1)S(1)}, u32[]{:S(2)}, u32[]{:S(2)}) collective-permute-start(bf16[2,208,640]{2,1,0:T(8,128)(2,1)S(1)} %get-tuple-element.54), channel_id=1, source_target_pairs={{0,14},{4,0},{8,4},{12,8},{2,12},{6,2},{10,6},{14,10},{1,15},{5,1}... | collective-permute-start | bytes 1597448 | tf_op jit(solution)/shard_map/ppermute | solution.py:32
  95.2 21.0 %collective-permute-start.19 = (bf16[112,640]{1,0:T(8,128)(2,1)S(1)}, bf16[112,640]{1,0:T(8,128)(2,1)S(1)}, u32[]{:S(2)}, u32[]{:S(2)}) collective-permute-start(bf16[112,640]{1,0:T(8,128)(2,1)S(1)} %get-tuple-element.58), channel_id=1, source_target_pairs={{0,10},{4,14},{8,0},{12,4},{2,8},{6,12},{10,2},{14,6},{1,11},{5,15... | collective-permute-start | bytes 430088 | tf_op jit(solution)/shard_map/ppermute | solution.py:32
  100.6 15.6 %collective-permute-start.18 = (bf16[96,640]{1,0:T(8,128)(2,1)S(1)}, bf16[96,640]{1,0:T(8,128)(2,1)S(1)}, u32[]{:S(2)}, u32[]{:S(2)}) collective-permute-start(bf16[96,640]{1,0:T(8,128)(2,1)S(1)} %get-tuple-element.57), channel_id=1, source_target_pairs={{0,8},{4,12},{8,2},{12,6},{2,10},{6,14},{10,0},{14,4},{1,9},{5,13}... | collective-permute-start | bytes 368648 | tf_op jit(solution)/shard_map/ppermute | solution.py:32
  116.4 4.7 %collective-permute-start.22 = (bf16[2,160,640]{2,1,0:T(8,128)(2,1)S(1)}, bf16[2,160,640]{2,1,0:T(8,128)(2,1)}, u32[]{:S(2)}, u32[]{:S(2)}) collective-permute-start(bf16[2,160,640]{2,1,0:T(8,128)(2,1)S(1)} %get-tuple-element.64), channel_id=1, source_target_pairs={{0,1},{1,0},{2,3},{3,2},{4,5},{5,4},{6,7},{7,6},{8,9},{9,8},{10,11... | collective-permute-start | bytes 1228808 | tf_op jit(solution)/shard_map/ppermute | solution.py:36
  116.5 5.9 %collective-permute-start.23 = (bf16[2,160,640]{2,1,0:T(8,128)(2,1)S(1)}, bf16[2,160,640]{2,1,0:T(8,128)(2,1)}, u32[]{:S(2)}, u32[]{:S(2)}) collective-permute-start(bf16[2,160,640]{2,1,0:T(8,128)(2,1)S(1)} %collective-permute-done.10), channel_id=1, source_target_pairs={{0,1},{1,0},{2,3},{3,2},{4,5},{5,4},{6,7},{7,6},{8,9},{9,8},{10,11... | collective-permute-start | bytes 1228808 | tf_op jit(solution)/shard_map/ppermute | solution.py:36
  117.0 11.5 %collective-permute-start.20 = (bf16[208,640]{1,0:T(8,128)(2,1)S(1)}, bf16[208,640]{1,0:T(8,128)(2,1)S(1)}, u32[]{:S(2)}, u32[]{:S(2)}) collective-permute-start(bf16[208,640]{1,0:T(8,128)(2,1)S(1)} %get-tuple-element.62), channel_id=1, source_target_pairs={{0,8},{4,12},{8,2},{12,6},{2,10},{6,14},{10,0},{14,4},{1,9},{5,13}... | collective-permute-start | bytes 798728 | tf_op jit(solution)/shard_map/ppermute | solution.py:32
  119.6 9.2 %collective-permute-start.21 = (bf16[208,640]{1,0:T(8,128)(2,1)S(1)}, bf16[208,640]{1,0:T(8,128)(2,1)S(1)}, u32[]{:S(2)}, u32[]{:S(2)}) collective-permute-start(bf16[208,640]{1,0:T(8,128)(2,1)S(1)} %get-tuple-element.63), channel_id=1, source_target_pairs={{0,10},{4,14},{8,0},{12,4},{2,8},{6,12},{10,2},{14,6},{1,11},{5,15... | collective-permute-start | bytes 798728 | tf_op jit(solution)/shard_map/ppermute | solution.py:32
  129.7 12.9 %collective-permute-start.25 = (bf16[160,640]{1,0:T(8,128)(2,1)S(1)}, bf16[160,640]{1,0:T(8,128)(2,1)S(1)}, u32[]{:S(2)}, u32[]{:S(2)}) collective-permute-start(bf16[160,640]{1,0:T(8,128)(2,1)S(1)} %get-tuple-element.67.l0), channel_id=1, source_target_pairs={{0,14},{14,0},{4,8},{8,4},{12,2},{2,12},{10,6},{6,10},{24,20},{20,... | collective-permute-start | bytes 614408 | tf_op jit(solution)/shard_map/ppermute | solution.py:321
  138.3 4.5 %collective-permute-start.24 = (bf16[160,640]{1,0:T(8,128)(2,1)S(1)}, bf16[160,640]{1,0:T(8,128)(2,1)S(1)}, u32[]{:S(2)}, u32[]{:S(2)}) collective-permute-start(bf16[160,640]{1,0:T(8,128)(2,1)S(1)} %get-tuple-element.67.l0), channel_id=1, source_target_pairs={{0,1},{1,0},{2,3},{3,2},{4,5},{5,4},{6,7},{7,6},{8,9},{9,8},{10,11... | collective-permute-start | bytes 614408 | tf_op jit(solution)/shard_map/ppermute | solution.py:36
  138.3 11.7 %collective-permute-start.27 = (f32[20,640]{1,0:T(8,128)S(1)}, f32[20,640]{1,0:T(8,128)S(1)}, u32[]{:S(2)}, u32[]{:S(2)}) collective-permute-start(f32[20,640]{1,0:T(8,128)S(1)} %get-tuple-element.68), channel_id=1, source_target_pairs={{0,0},{14,2},{4,4},{8,6},{12,32},{2,34},{10,36},{6,38},{24,8},{20,... | collective-permute-start | bytes 153608 | tf_op jit(solution)/shard_map/ppermute | solution.py:322
  142.5 1.5 collective-permute-start.26
  150.0 14.0 %collective-permute-start.28 = (bf16[160,640]{1,0:T(8,128)(2,1)S(1)}, bf16[160,640]{1,0:T(8,128)(2,1)S(1)}, u32[]{:S(2)}, u32[]{:S(2)}) collective-permute-start(bf16[160,640]{1,0:T(8,128)(2,1)S(1)} %shard_map.90), channel_id=1, source_target_pairs={{0,0},{14,2},{4,4},{8,6},{12,32},{2,34},{10,36},{6,38},{24,8},{20,... | collective-permute-start | bytes 614408 | tf_op jit(solution)/shard_map/ppermute | solution.py:337
